TPU v7x, 512 devices: a whole 4x4x16 slice. The times are simulated.
512 devices in a mesh: lat: 64 (over x, z_lo, core), lon: 8 (over z_hi, y).
Axes of the slice: x: 4, y: 4, z: 16 (z_hi: 2, z_lo: 8; z = z_hi * 8 + z_lo), core: 2. Of those that a mesh axis runs over, the one named last changes fastest.
Arguments:
- fine_field: bfloat16 [1, 768, 1440, 128], P(None, 'lat', 'lon'), may hold values from -6 to 6
- conv_first: bfloat16 [3, 3, 128, 128], replicated, may hold values from -0.1875 to 0.1875
- bias_first: float32 [128], replicated, may hold values from -3 to 3
- film_terms: float32 [2, 128], replicated, may hold values from -0.5 to 0.5
- conv_second: bfloat16 [3, 3, 128, 128], replicated, may hold values from -0.1875 to 0.1875
- bottleneck_in: bfloat16 [1, 3072, 1024], P(None, 'lat', 'lon'), may hold values from -6 to 6
- query_weight: bfloat16 [1024, 1024], P(None, 'lon')
- key_weight: bfloat16 [1024, 1024], P(None, 'lon')
- value_weight: bfloat16 [1024, 1024], P(None, 'lon'), may hold values from -0.1875 to 0.1875
- out_weight: bfloat16 [1024, 1024], P('lon'), may hold values from -1 to 1
Outputs:
- fine_out: bfloat16 [1, 768, 1440, 128], P(None, 'lat', 'lon')
- bottleneck_out: bfloat16 [1, 3072, 1024], P(None, 'lat', 'lon')
All inputs are finite; a program needn't handle non-finite values.
Results may differ from a plain program's by a relative error of at most 0.018.
Values may be sent and summed in bfloat16 or wider, within the bound.
No kernel may reach another device: no remote copies, remote signals or barrier semaphores. Data moves between devices by JAX's collectives and lax.ppermute only.
A program may use at most 64 MiB of HBM per device.

v0:
```python
import math

import jax
import jax.numpy as jnp
from jax import lax
from jax.sharding import PartitionSpec as P

HEAD = 64


def extended(shard, sides, width, wrap):
    for axis, dim in sides:
        count, length = (lax.axis_size(axis), shard.shape[dim])
        up = [(i, (i + 1) % count) for i in range(count if wrap else count - 1)]
        down = [(j, i) for i, j in up]
        last = lax.slice_in_dim(shard, length - width, length, axis=dim)
        initial = lax.slice_in_dim(shard, 0, width, axis=dim)
        before = lax.ppermute(last, axis, up)
        after = lax.ppermute(initial, axis, down)
        shard = jnp.concatenate([before, shard, after], axis=dim)
    return shard


def from_behind(shard, axis, by):
    count = lax.axis_size(axis)
    return lax.ppermute(shard, axis, [(i, (i + by) % count) for i in range(count)])


def conv_valid(padded, kernel):
    return lax.conv_general_dilated(
        padded,
        kernel,
        (1, 1),
        "VALID",
        dimension_numbers=("NHWC", "HWIO", "NHWC"),
        preferred_element_type=jnp.float32,
    )


def project(inputs, weight):
    return jnp.einsum("mtd,de->mte", inputs, weight, preferred_element_type=jnp.float32).astype(
        jnp.bfloat16
    )


def shards(
    fine_field,
    conv_first,
    bias_first,
    film_terms,
    conv_second,
    bottleneck_in,
    query_weight,
    key_weight,
    value_weight,
    out_weight,
):
    lat_count = lax.axis_size("lat")
    lat_place = lax.axis_index("lat")
    half_turn = lax.axis_size("lon") // 2

    def pole_pad(field):
        rimmed = extended(field, (("lat", 1),), 1, False)
        edges = jnp.concatenate([field[:, :1], field[:, -1:]], axis=1)
        turned = from_behind(edges, "lon", half_turn)
        top_rows = jnp.where(lat_place == 0, turned[:, :1], rimmed[:, :1])
        bottom_rows = jnp.where(lat_place == lat_count - 1, turned[:, 1:], rimmed[:, -1:])
        lat_padded = jnp.concatenate([top_rows, field, bottom_rows], axis=1)
        return extended(lat_padded, (("lon", 2),), 1, True)

    first = conv_valid(pole_pad(fine_field), conv_first)
    hidden = jax.nn.silu((first + bias_first) * (1.0 + film_terms[0]) + film_terms[1]).astype(
        jnp.bfloat16
    )
    second = conv_valid(pole_pad(hidden), conv_second)
    fine_out = (fine_field.astype(jnp.float32) + second).astype(jnp.bfloat16)
    gathered = lax.all_gather(bottleneck_in, "lon", axis=2, tiled=True)
    wide = gathered.astype(jnp.float32)
    normed = (wide * lax.rsqrt(jnp.mean(wide * wide, axis=-1, keepdims=True) + 1e-06)).astype(
        jnp.bfloat16
    )
    members = normed.shape[0]
    rows_here = normed.shape[1]
    local_width = query_weight.shape[1]
    heads_here = local_width // HEAD
    score_scale = 1.0 / math.sqrt(HEAD)
    queries_flat = project(normed, query_weight)
    queries = queries_flat.reshape(members, rows_here, heads_here, HEAD)
    rows_piece = lax.all_gather(normed, "lat", axis=1, tiled=True)
    keys_flat = project(rows_piece, key_weight)
    running_max = jnp.full((members, heads_here, rows_here), -jnp.inf, jnp.float32)
    running_sum = jnp.zeros((members, heads_here, rows_here), jnp.float32)
    running_acc = jnp.zeros((members, heads_here, rows_here, HEAD), jnp.float32)
    count = keys_flat.shape[1]
    keys_piece = keys_flat.reshape(members, count, heads_here, HEAD)
    values_piece = project(rows_piece, value_weight).reshape(members, count, heads_here, HEAD)
    scores = (
        jnp.einsum("mqhd,mkhd->mhqk", queries, keys_piece, preferred_element_type=jnp.float32)
        * score_scale
    )
    new_max = jnp.max(scores, axis=-1)
    factor = jnp.exp(running_max - new_max)
    expo = jnp.exp(scores - new_max[..., None])
    new_sum = running_sum * factor + jnp.sum(expo, axis=-1)
    new_acc = running_acc * factor[..., None] + jnp.einsum(
        "mhqk,mkhd->mhqd",
        expo.astype(jnp.bfloat16),
        values_piece,
        preferred_element_type=jnp.float32,
    )
    attended = (
        (new_acc / new_sum[..., None])
        .transpose(0, 2, 1, 3)
        .reshape(members, rows_here, local_width)
        .astype(jnp.bfloat16)
    )
    partial_out = jnp.einsum(
        "mth,hd->mtd", attended, out_weight, preferred_element_type=jnp.float32
    )
    shared = lax.psum_scatter(
        partial_out.astype(jnp.bfloat16), "lon", scatter_dimension=2, tiled=True
    ).astype(jnp.float32)
    bottleneck_out = (bottleneck_in.astype(jnp.float32) + shared).astype(jnp.bfloat16)
    return (fine_out, bottleneck_out)


def solution(mesh):
    placed = (
        P(None, "lat", "lon", None),
        P(),
        P(),
        P(),
        P(),
        P(None, "lat", "lon"),
        P(None, "lon"),
        P(None, "lon"),
        P(None, "lon"),
        P("lon", None),
    )
    return jax.shard_map(
        shards,
        mesh=mesh,
        in_specs=placed,
        out_specs=(P(None, "lat", "lon", None), P(None, "lat", "lon")),
        check_vma=False,
    )
```

profile of v0, /device:TPU:1, one launch (start us, length us, event | category | flops | bytes accessed | tf_op | source)
XLA Modules:
  0.0 324.1 jit_solution(1224849192424416516)
XLA Ops:
  7.2 59.7 %all_gather.6 = bf16[1,48,1024]{2,1,0:T(8,128)(2,1)S(1)} all-gather(bf16[1,48,128]{2,1,0:T(8,128)(2,1)} %param.15), channel_id=1, replica_groups=mesh['lat'=64,'lon'=8] {'lon'}, dimensions={2}, use_global_device_ids=true | all-gather | bytes 110592 | tf_op jit(solution)/shard_map/all_gather | solution.py:77
  66.9 0.1 fusion.39
  67.0 0.7 fusion.40
  67.8 0.8 fusion.51
  68.7 10.9 %collective-permute-start = (bf16[1,2,180,128]{3,2,1,0:T(8,128)(2,1)S(1)}, bf16[1,2,180,128]{3,2,1,0:T(8,128)(2,1)S(1)}, u32[]{:S(2)}, u32[]{:S(2)}) collective-permute-start(bf16[1,2,180,128]{3,2,1,0:T(8,128)(2,1)S(1)} %pad_maximum_fusion), channel_id=1, source_target_pairs={{0,4},{1,5},{2,6},{3,7},{4,0},{5,1},{6,2},{7,3},{8,12},{9,13},{10,... | collective-permute-start | bytes 276488 | tf_op jit(solution)/shard_map/ppermute | solution.py:26
  79.6 8.2 %collective-permute-start.1 = (bf16[1,1,180,128]{3,2,1,0:T(8,128)(2,1)S(1)}, bf16[1,1,180,128]{3,2,1,0:T(8,128)(2,1)S(1)}, u32[]{:S(2)}, u32[]{:S(2)}) collective-permute-start(bf16[1,1,180,128]{3,2,1,0:T(8,128)(2,1)S(1)} %get-tuple-element.8), channel_id=1, source_target_pairs={{0,8},{8,16},{16,24},{24,32},{32,40},{40,48},{48,56},{56,64},{64,7... | collective-permute-start | bytes 138248 | tf_op jit(solution)/shard_map/ppermute | solution.py:18
  87.8 1.9 collective-permute-start.2
  89.8 4.0 %collective-permute-done.2 = bf16[1,1,180,128]{3,2,1,0:T(8,128)(2,1)S(1)} collective-permute-done((bf16[1,1,180,128]{3,2,1,0:T(8,128)(2,1)S(1)}, bf16[1,1,180,128]{3,2,1,0:T(8,128)(2,1)S(1)}, u32[]{:S(2)}, u32[]{:S(2)}) %collective-permute-start.2) | collective-permute-done | bytes 46112 | tf_op jit(solution)/shard_map/ppermute | solution.py:19
  93.9 1.9 collective-permute-start.4
  95.8 3.4 %collective-permute-start.3 = (bf16[1,14,1,128]{3,2,1,0:T(2,128)(2,1)S(1)}, bf16[1,14,1,128]{3,2,1,0:T(2,128)(2,1)S(1)}, u32[]{:S(2)}, u32[]{:S(2)}) collective-permute-start(bf16[1,14,1,128]{3,2,1,0:T(2,128)(2,1)S(1)} %get-tuple-element.4), channel_id=1, source_target_pairs={{0,1},{1,2},{2,3},{3,4},{4,5},{5,6},{6,7},{7,0},{8,9},{9,10},{10,1... | collective-permute-start | bytes 10760 | tf_op jit(solution)/shard_map/ppermute | solution.py:18
  99.2 11.9 %collective-permute-done.3 = bf16[1,14,1,128]{3,2,1,0:T(2,128)(2,1)S(1)} collective-permute-done((bf16[1,14,1,128]{3,2,1,0:T(2,128)(2,1)S(1)}, bf16[1,14,1,128]{3,2,1,0:T(2,128)(2,1)S(1)}, u32[]{:S(2)}, u32[]{:S(2)}) %collective-permute-start.3) | collective-permute-done | bytes 3616 | tf_op jit(solution)/shard_map/ppermute | solution.py:18
  111.1 0.2 maximum_bitcast_fusion
  111.4 0.2 reshape.122
  111.6 0.1 copy.25
  111.8 0.3 copy-done.11
  112.1 1.7 multiply_convert_fusion
  113.7 0.1 copy.28
  113.9 9.3 %collective-permute-start.6 = (bf16[1,1,180,128]{3,2,1,0:T(8,128)(2,1)S(1)}, bf16[1,1,180,128]{3,2,1,0:T(8,128)(2,1)S(1)}, u32[]{:S(2)}, u32[]{:S(2)}) collective-permute-start(bf16[1,1,180,128]{3,2,1,0:T(8,128)(2,1)S(1)} %bitcast.73), channel_id=1, source_target_pairs={{0,8},{8,16},{16,24},{24,32},{32,40},{40,48},{48,56},{56,64},{64,7... | collective-permute-start | bytes 138248 | tf_op jit(solution)/shard_map/ppermute | solution.py:18
  123.4 6.1 %collective-permute-start.5 = (bf16[1,2,180,128]{3,2,1,0:T(8,128)(2,1)S(1)}, bf16[1,2,180,128]{3,2,1,0:T(8,128)(2,1)S(1)}, u32[]{:S(2)}, u32[]{:S(2)}) collective-permute-start(bf16[1,2,180,128]{3,2,1,0:T(8,128)(2,1)S(1)} %slice_bitcast_fusion.2), channel_id=1, source_target_pairs={{0,4},{1,5},{2,6},{3,7},{4,0},{5,1},{6,2},{7,3},{8,12},{9,13},{10,... | collective-permute-start | bytes 276488 | tf_op jit(solution)/shard_map/ppermute | solution.py:26
  129.6 1.9 collective-permute-start.7
  131.5 0.2 reshape.137
  131.8 7.3 %collective-permute-done.7 = bf16[1,1,180,128]{3,2,1,0:T(8,128)(2,1)S(1)} collective-permute-done((bf16[1,1,180,128]{3,2,1,0:T(8,128)(2,1)S(1)}, bf16[1,1,180,128]{3,2,1,0:T(8,128)(2,1)S(1)}, u32[]{:S(2)}, u32[]{:S(2)}) %collective-permute-start.7) | collective-permute-done | bytes 46112 | tf_op jit(solution)/shard_map/ppermute | solution.py:19
  139.0 3.5 %collective-permute-done.5 = bf16[1,2,180,128]{3,2,1,0:T(8,128)(2,1)S(1)} collective-permute-done((bf16[1,2,180,128]{3,2,1,0:T(8,128)(2,1)S(1)}, bf16[1,2,180,128]{3,2,1,0:T(8,128)(2,1)S(1)}, u32[]{:S(2)}, u32[]{:S(2)}) %collective-permute-start.5) | collective-permute-done | bytes 92192 | tf_op jit(solution)/shard_map/ppermute | solution.py:26
  142.5 1.9 collective-permute-start.9
  144.5 3.4 %collective-permute-start.8 = (bf16[1,14,1,128]{3,2,1,0:T(2,128)(2,1)S(1)}, bf16[1,14,1,128]{3,2,1,0:T(2,128)(2,1)S(1)}, u32[]{:S(2)}, u32[]{:S(2)}) collective-permute-start(bf16[1,14,1,128]{3,2,1,0:T(2,128)(2,1)S(1)} %get-tuple-element.2), channel_id=1, source_target_pairs={{0,1},{1,2},{2,3},{3,4},{4,5},{5,6},{6,7},{7,0},{8,9},{9,10},{10,1... | collective-permute-start | bytes 10760 | tf_op jit(solution)/shard_map/ppermute | solution.py:18
  147.8 0.2 convolution_convert_fusion.1
  148.1 11.7 %collective-permute-done.8 = bf16[1,14,1,128]{3,2,1,0:T(2,128)(2,1)S(1)} collective-permute-done((bf16[1,14,1,128]{3,2,1,0:T(2,128)(2,1)S(1)}, bf16[1,14,1,128]{3,2,1,0:T(2,128)(2,1)S(1)}, u32[]{:S(2)}, u32[]{:S(2)}) %collective-permute-start.8) | collective-permute-done | bytes 3616 | tf_op jit(solution)/shard_map/ppermute | solution.py:18
  159.8 0.2 maximum_bitcast_fusion.1
  160.0 0.2 reshape.133
  160.3 0.1 copy.31
  160.4 0.6 copy-done.10
  161.0 1.5 convolution_select_fusion
  162.5 0.2 copy.32
  162.8 38.7 %all-gather.2.cloned.1.call-done = bf16[1,3072,1024]{2,1,0:T(8,128)(2,1)} async-done(((bf16[1,48,1024]{2,1,0:T(8,128)(2,1)}), bf16[1,3072,1024]{2,1,0:T(8,128)(2,1)}) %all-gather.2.cloned.1.call-update) | async-done | bytes 6291472 | tf_op jit(solution)/shard_map/all_gather | solution.py:89
  201.5 5.1 %fusion.4 = bf16[3072,128]{0,1:T(8,128)(2,1)S(1)} fusion(bf16[1024,128]{1,0:T(8,128)(2,1)S(1)} %copy-done.4, bf16[1,3072,1024]{2,1,0:T(8,128)(2,1)} %all-gather.2.cloned.1.call-done), kind=kOutput, calls=%fused_computation.5 | convolution fusion | flops 805699584 | bytes 7340032 | tf_op jit(solution)/shard_map/mtd,de->mte/dot_general | solution.py:41
  206.7 0.4 fusion.52
  207.1 0.3 fusion.21
  207.4 0.2 copy-done.5
  207.6 2.2 fusion.7
  209.8 0.4 fusion.20
  210.4 0.4 copy-done.7
  210.8 0.2 fusion.17
  210.9 0.4 copy.35
  211.3 0.7 copy.43
  212.1 1.0 fusion.16
  213.1 102.7 %reduce-scatter.4.cloned.1.call-done = bf16[128,48]{1,0:T(8,128)(2,1)} async-done(((bf16[1024,48]{1,0:T(8,128)(2,1)}), bf16[128,48]{1,0:T(8,128)(2,1)}) %reduce-scatter.4.cloned.1.call-update) | async-done | bytes 12304
  315.7 0.8 reshape_bitcast_fusion
  316.6 0.6 add_convert_fusion
  (58 shorter events, 1.1 us)
Async XLA Ops:
  7.2 104.6 %copy-start = (bf16[3,3,128,128]{3,2,1,0:T(8,128)(2,1)S(1)}, bf16[3,3,128,128]{3,2,1,0:T(8,128)(2,1)}, u32[]{:S(2)}) copy-start(bf16[3,3,128,128]{3,2,1,0:T(8,128)(2,1)} %param.11) | copy-start | bytes 884740
  7.2 86.7 %copy-start.2 = (bf16[1,12,180,128]{3,2,1,0:T(8,128)(2,1)S(1)}, bf16[1,12,180,128]{3,2,1,0:T(8,128)(2,1)}, u32[]{:S(2)}) copy-start(bf16[1,12,180,128]{3,2,1,0:T(8,128)(2,1)} %param.10) | copy-start | bytes 1658884
  7.2 92.0 %copy-start.9 = (f32[2,128]{1,0:T(2,128)S(1)}, f32[2,128]{1,0:T(2,128)}, u32[]{:S(2)}) copy-start(f32[2,128]{1,0:T(2,128)} %param.13) | copy-start | bytes 3076
  7.2 194.3 %all-gather.2.cloned.1.call-start = ((), (), s32[]{:S(2)}) async-start(), calls=%async_computation.1 | async-start | bytes 6389760 | tf_op jit(solution)/shard_map/all_gather | solution.py:89
  67.8 247.9 %reduce-scatter.4.cloned.1.call-start = ((), (), s32[]{:S(2)}) async-start(), calls=%async_computation.2 | async-start | bytes 294912
  68.7 25.1 %collective-permute-start = (bf16[1,2,180,128]{3,2,1,0:T(8,128)(2,1)S(1)}, bf16[1,2,180,128]{3,2,1,0:T(8,128)(2,1)S(1)}, u32[]{:S(2)}, u32[]{:S(2)}) collective-permute-start(bf16[1,2,180,128]{3,2,1,0:T(8,128)(2,1)S(1)} %pad_maximum_fusion), channel_id=1, source_target_pairs={{0,4},{1,5},{2,6},{3,7},{4,0},{5,1},{6,2},{7,3},{8,12},{9,13},{10,... | collective-permute-start | bytes 276488 | tf_op jit(solution)/shard_map/ppermute | solution.py:26
  79.6 10.1 %collective-permute-start.1 = (bf16[1,1,180,128]{3,2,1,0:T(8,128)(2,1)S(1)}, bf16[1,1,180,128]{3,2,1,0:T(8,128)(2,1)S(1)}, u32[]{:S(2)}, u32[]{:S(2)}) collective-permute-start(bf16[1,1,180,128]{3,2,1,0:T(8,128)(2,1)S(1)} %get-tuple-element.8), channel_id=1, source_target_pairs={{0,8},{8,16},{16,24},{24,32},{32,40},{40,48},{48,56},{56,64},{64,7... | collective-permute-start | bytes 138248 | tf_op jit(solution)/shard_map/ppermute | solution.py:18
  87.8 6.0 %collective-permute-start.2 = (bf16[1,1,180,128]{3,2,1,0:T(8,128)(2,1)S(1)}, bf16[1,1,180,128]{3,2,1,0:T(8,128)(2,1)S(1)}, u32[]{:S(2)}, u32[]{:S(2)}) collective-permute-start(bf16[1,1,180,128]{3,2,1,0:T(8,128)(2,1)S(1)} %get-tuple-element.9), channel_id=1, source_target_pairs={{8,0},{16,8},{24,16},{32,24},{40,32},{48,40},{56,48},{64,56},{72,6... | collective-permute-start | bytes 138248 | tf_op jit(solution)/shard_map/ppermute | solution.py:19
  93.9 5.3 %collective-permute-start.4 = (bf16[1,14,1,128]{3,2,1,0:T(2,128)(2,1)S(1)}, bf16[1,14,1,128]{3,2,1,0:T(2,128)(2,1)S(1)}, u32[]{:S(2)}, u32[]{:S(2)}) collective-permute-start(bf16[1,14,1,128]{3,2,1,0:T(2,128)(2,1)S(1)} %get-tuple-element.5), channel_id=1, source_target_pairs={{1,0},{2,1},{3,2},{4,3},{5,4},{6,5},{7,6},{0,7},{9,8},{10,9},{11,1... | collective-permute-start | bytes 10760 | tf_op jit(solution)/shard_map/ppermute | solution.py:19
  95.8 15.3 %collective-permute-start.3 = (bf16[1,14,1,128]{3,2,1,0:T(2,128)(2,1)S(1)}, bf16[1,14,1,128]{3,2,1,0:T(2,128)(2,1)S(1)}, u32[]{:S(2)}, u32[]{:S(2)}) collective-permute-start(bf16[1,14,1,128]{3,2,1,0:T(2,128)(2,1)S(1)} %get-tuple-element.4), channel_id=1, source_target_pairs={{0,1},{1,2},{2,3},{3,4},{4,5},{5,6},{6,7},{7,0},{8,9},{9,10},{10,1... | collective-permute-start | bytes 10760 | tf_op jit(solution)/shard_map/ppermute | solution.py:18
  111.4 0.7 copy-start.11
  111.4 0.7 copy-start.12
  113.9 17.8 %collective-permute-start.6 = (bf16[1,1,180,128]{3,2,1,0:T(8,128)(2,1)S(1)}, bf16[1,1,180,128]{3,2,1,0:T(8,128)(2,1)S(1)}, u32[]{:S(2)}, u32[]{:S(2)}) collective-permute-start(bf16[1,1,180,128]{3,2,1,0:T(8,128)(2,1)S(1)} %bitcast.73), channel_id=1, source_target_pairs={{0,8},{8,16},{16,24},{24,32},{32,40},{40,48},{48,56},{56,64},{64,7... | collective-permute-start | bytes 138248 | tf_op jit(solution)/shard_map/ppermute | solution.py:18
  123.4 19.1 %collective-permute-start.5 = (bf16[1,2,180,128]{3,2,1,0:T(8,128)(2,1)S(1)}, bf16[1,2,180,128]{3,2,1,0:T(8,128)(2,1)S(1)}, u32[]{:S(2)}, u32[]{:S(2)}) collective-permute-start(bf16[1,2,180,128]{3,2,1,0:T(8,128)(2,1)S(1)} %slice_bitcast_fusion.2), channel_id=1, source_target_pairs={{0,4},{1,5},{2,6},{3,7},{4,0},{5,1},{6,2},{7,3},{8,12},{9,13},{10,... | collective-permute-start | bytes 276488 | tf_op jit(solution)/shard_map/ppermute | solution.py:26
  129.6 9.5 %collective-permute-start.7 = (bf16[1,1,180,128]{3,2,1,0:T(8,128)(2,1)S(1)}, bf16[1,1,180,128]{3,2,1,0:T(8,128)(2,1)S(1)}, u32[]{:S(2)}, u32[]{:S(2)}) collective-permute-start(bf16[1,1,180,128]{3,2,1,0:T(8,128)(2,1)S(1)} %bitcast.74), channel_id=1, source_target_pairs={{8,0},{16,8},{24,16},{32,24},{40,32},{48,40},{56,48},{64,56},{72,6... | collective-permute-start | bytes 138248 | tf_op jit(solution)/shard_map/ppermute | solution.py:19
  131.7 16.2 %copy-start.3 = (bf16[1,48,1024]{2,1,0:T(8,128)(2,1)S(1)}, bf16[1,48,1024]{2,1,0:T(8,128)(2,1)}, u32[]{:S(2)}) copy-start(bf16[1,48,1024]{2,1,0:T(8,128)(2,1)} %fusion.40) | copy-start | bytes 294916
  131.7 16.2 %copy-start.6 = (bf16[1024,128]{1,0:T(8,128)(2,1)S(1)}, bf16[1024,128]{1,0:T(8,128)(2,1)}, u32[]{:S(2)}) copy-start(bf16[1024,128]{1,0:T(8,128)(2,1)} %param.16) | copy-start | bytes 786436
  142.5 5.6 %collective-permute-start.9 = (bf16[1,14,1,128]{3,2,1,0:T(2,128)(2,1)S(1)}, bf16[1,14,1,128]{3,2,1,0:T(2,128)(2,1)S(1)}, u32[]{:S(2)}, u32[]{:S(2)}) collective-permute-start(bf16[1,14,1,128]{3,2,1,0:T(2,128)(2,1)S(1)} %get-tuple-element.3), channel_id=1, source_target_pairs={{1,0},{2,1},{3,2},{4,3},{5,4},{6,5},{7,6},{0,7},{9,8},{10,9},{11,1... | collective-permute-start | bytes 10760 | tf_op jit(solution)/shard_map/ppermute | solution.py:19
  144.5 15.3 %collective-permute-start.8 = (bf16[1,14,1,128]{3,2,1,0:T(2,128)(2,1)S(1)}, bf16[1,14,1,128]{3,2,1,0:T(2,128)(2,1)S(1)}, u32[]{:S(2)}, u32[]{:S(2)}) collective-permute-start(bf16[1,14,1,128]{3,2,1,0:T(2,128)(2,1)S(1)} %get-tuple-element.2), channel_id=1, source_target_pairs={{0,1},{1,2},{2,3},{3,4},{4,5},{5,6},{6,7},{7,0},{8,9},{9,10},{10,1... | collective-permute-start | bytes 10760 | tf_op jit(solution)/shard_map/ppermute | solution.py:18
  160.0 1.0 copy-start.10
  162.7 38.8 %copy-start.4 = (bf16[1024,128]{1,0:T(8,128)(2,1)S(1)}, bf16[1024,128]{1,0:T(8,128)(2,1)}, u32[]{:S(2)}) copy-start(bf16[1024,128]{1,0:T(8,128)(2,1)} %param.17) | copy-start | bytes 786436
  201.5 5.9 %copy-start.1 = (bf16[1,3072,1024]{2,1,0:T(8,128)(2,1)S(1)}, bf16[1,3072,1024]{2,1,0:T(8,128)(2,1)}, u32[]{:S(2)}) copy-start(bf16[1,3072,1024]{2,1,0:T(8,128)(2,1)} %all-gather.2.cloned.1.call-done) | copy-start | bytes 18874372
  206.7 1.0 copy-start.5
  209.8 1.0 copy-start.7
  212.1 104.5 %copy-start.8 = (bf16[1,48,128]{2,1,0:T(8,128)(2,1)S(1)}, bf16[1,48,128]{2,1,0:T(8,128)(2,1)}, u32[]{:S(2)}) copy-start(bf16[1,48,128]{2,1,0:T(8,128)(2,1)} %param.15) | copy-start | bytes 36868
Sparse Core Ops, SparseCore 0:
  67.9 133.5 all-gather.1
  212.2 103.4 reduce-scatter.3
where the time goes:
time: 325 us; the launch traced here: 324 us
  waiting for transfers between devices  180 us (55%)
  blocking collectives  59.7 us (18%)
  starting transfers between devices  49.1 us (15%)
  between operations  14.6 us (4%)
  matrix products  11.7 us (4%)
  local copies, waits for them, and re-layouts  6.16 us (2%)
  other arithmetic  3.28 us (1%)
    unnamed x3, waiting for transfers between devices  103 us
    all_gather x1, blocking collectives, shards(): gathered = lax.all_gather(bottleneck_in, 'lon', axis=2, tiled=True)  59.7 us
    all_gather x1, waiting for transfers between devices, shards(): rows_piece = lax.all_gather(normed, 'lat', axis=1, tiled=True)  38.7 us
    ppermute x4, starting transfers between devices, extended(): before = lax.ppermute(last, axis, up)  24.2 us
    ppermute x4, waiting for transfers between devices, extended(): before = lax.ppermute(last, axis, up)  23.6 us
    ppermute x2, starting transfers between devices, from_behind(): lax.ppermute(shard, axis, [(i, (i + by) % count) for i in range(count)])  17 us
    ppermute x4, waiting for transfers between devices, extended(): after = lax.ppermute(initial, axis, down)  11.3 us
    ppermute x4, starting transfers between devices, extended(): after = lax.ppermute(initial, axis, down)  7.68 us
  transfers between devices with their start and end apart: 12, of which 7 were waited for; matrix products, arithmetic and copies ran while one was open for 2% of the time, Pallas kernels for 0%

commit v1 on v0

v1 whole, which is shorter than its diff:
```python
import functools

import jax
import jax.numpy as jnp
from jax import lax
from jax.experimental import pallas as pl
from jax.experimental.pallas import tpu as pltpu
from jax.sharding import PartitionSpec as P

HEAD = 64
BF16 = jnp.bfloat16
F32 = jnp.float32
VMEM_LIMIT = 48 * 1024 * 1024


def lat_groups():
    place = lambda x, z, c: x * 16 + z * 2 + c
    over_z = [[place(x, z, c) for z in range(8)] for x in range(4) for c in range(2)]
    over_xc = [[place(x, z, c) for x in range(4) for c in range(2)] for z in range(8)]
    return over_z, over_xc


def halo_pairs(lat, lon):
    inner, outer = [], []
    for i in range(lat):
        for j in range(lon):
            me = i * lon + j
            inner.append((me, (i ^ 1) * lon + j))
            if i in (0, lat - 1):
                outer.append((me, i * lon + (j + lon // 2) % lon))
            else:
                outer.append((me, (i + 1 if i % 2 else i - 1) * lon + j))
    return inner, outer


def kernel_call(body, out_shape, **extra):
    return pl.pallas_call(
        body,
        out_shape=out_shape,
        compiler_params=pltpu.CompilerParams(vmem_limit_bytes=VMEM_LIMIT),
        **extra,
    )


def project_body(tokens_ref, wq_ref, wk_ref, wv_ref, q_ref, kv_ref):
    rows = q_ref.shape[1]
    wide = jnp.concatenate([tokens_ref[j, :rows, :] for j in range(tokens_ref.shape[0])], axis=1).astype(F32)
    normed = (wide * lax.rsqrt(jnp.mean(wide * wide, axis=-1, keepdims=True) + 1e-06)).astype(BF16)
    q = jnp.dot(normed, wq_ref[...], preferred_element_type=F32).astype(BF16)
    k = jnp.dot(normed, wk_ref[...], preferred_element_type=F32).astype(BF16)
    v = jnp.dot(normed, wv_ref[...], preferred_element_type=F32).astype(BF16)
    kv = jnp.concatenate([k, v], axis=1)
    for j in range(q_ref.shape[0]):
        q_ref[j] = q
    for j in range(kv_ref.shape[0]):
        kv_ref[j] = kv


def attend_body(q_ref, kv_ref, o_ref):
    n, rows, width = q_ref.shape
    q = q_ref[...].reshape(n * rows, width)
    kv = kv_ref[...].reshape(kv_ref.shape[0] * kv_ref.shape[1], 2 * width)
    scale = 1.0 / HEAD**0.5
    outs = []
    lane = lax.broadcasted_iota(jnp.int32, (n * rows, width), 1)
    tail = jnp.zeros((n * rows, width), F32)
    for h in range(width // HEAD):
        qh = q[:, h * HEAD : (h + 1) * HEAD]
        kh = kv[:, h * HEAD : (h + 1) * HEAD]
        vh = kv[:, width + h * HEAD : width + (h + 1) * HEAD]
        scores = lax.dot_general(qh, kh, (((1,), (1,)), ((), ())), preferred_element_type=F32) * scale
        top = jnp.max(scores, axis=-1, keepdims=True)
        expo = jnp.exp(scores - top)
        total = jnp.sum(expo, axis=-1, keepdims=True)
        outs.append(jnp.dot(expo.astype(BF16), vh, preferred_element_type=F32) / total)
        rest = top + jnp.log(total)
        for part in range(3):
            piece = rest.astype(BF16).astype(F32)
            rest = rest - piece
            tail = jnp.where(lane == 3 * h + part, piece, tail)
    o_ref[...] = jnp.concatenate(outs + [tail], axis=1).astype(BF16).reshape(o_ref.shape)


def merge_body(o_ref, wo_ref, out_ref):
    n, rows, width = o_ref.shape[0], o_ref.shape[1], o_ref.shape[2] // 2
    heads = []
    for h in range(width // HEAD):
        logs = []
        for p in range(n):
            pieces = o_ref[p, :, width : 2 * width].astype(F32)
            logs.append(pieces[:, 3 * h : 3 * h + 1] + pieces[:, 3 * h + 1 : 3 * h + 2] + pieces[:, 3 * h + 2 : 3 * h + 3])
        top = functools.reduce(jnp.maximum, logs)
        num = jnp.zeros((rows, HEAD), F32)
        total = jnp.zeros((rows, 1), F32)
        for p in range(n):
            weight = jnp.exp(logs[p] - top)
            total = total + weight
            num = num + weight * o_ref[p, :, h * HEAD : (h + 1) * HEAD].astype(F32)
        heads.append(num / total)
    attended = jnp.concatenate(heads, axis=1).astype(BF16)
    partial = jnp.dot(attended, wo_ref[...], preferred_element_type=F32).astype(BF16)
    for j in range(out_ref.shape[0]):
        out_ref[j] = partial[:, j * width : (j + 1) * width]


def finish_body(parts_ref, tokens_ref, out_ref):
    total = tokens_ref[...].astype(F32)
    shared = parts_ref[0].astype(F32)
    for j in range(1, parts_ref.shape[0]):
        shared = shared + parts_ref[j].astype(F32)
    out_ref[...] = (total + shared).astype(BF16)


def conv_valid(padded, kernel):
    return lax.conv_general_dilated(
        padded[None],
        kernel,
        (1, 1),
        "VALID",
        dimension_numbers=("NHWC", "HWIO", "NHWC"),
        preferred_element_type=F32,
    )[0]


def shards(
    fine_field,
    conv_first,
    bias_first,
    film_terms,
    conv_second,
    bottleneck_in,
    query_weight,
    key_weight,
    value_weight,
    out_weight,
):
    lats, lons = lax.axis_size("lat"), lax.axis_size("lon")
    lat, lon = lax.axis_index("lat"), lax.axis_index("lon")
    over_z, over_xc = lat_groups()
    inner, outer = halo_pairs(lats, lons)
    field, tokens = fine_field[0], bottleneck_in[0]
    height, width, channels = field.shape
    rows = tokens.shape[0]

    slot = jnp.arange(lons)[:, None, None]
    first_columns = field[:, :2].reshape(1, 2 * height, channels)
    last_columns = field[:, -2:].reshape(1, 2 * height, channels)
    columns = jnp.where(slot == (lon + 1) % lons, last_columns, first_columns)
    outgoing = jnp.concatenate([jnp.broadcast_to(tokens[None], (lons,) + tokens.shape), columns], axis=1)
    incoming = lax.all_to_all(outgoing, "lon", 0, 0)

    heads_width = query_weight.shape[1]
    n_z, n_xc = len(over_z[0]), len(over_xc[0])
    queries, pairs = kernel_call(
        project_body,
        (
            jax.ShapeDtypeStruct((n_xc, rows, heads_width), BF16),
            jax.ShapeDtypeStruct((n_z, rows, 2 * heads_width), BF16),
        ),
    )(incoming, query_weight, key_weight, value_weight)
    queries = lax.all_to_all(queries, "lat", 0, 0, axis_index_groups=over_xc)
    pairs = lax.all_to_all(pairs, "lat", 0, 0, axis_index_groups=over_z)

    before = lax.dynamic_index_in_dim(incoming, (lon + lons - 1) % lons, 0, False)[rows:].reshape(height, 2, channels)
    after = lax.dynamic_index_in_dim(incoming, (lon + 1) % lons, 0, False)[rows:].reshape(height, 2, channels)
    middle = jnp.concatenate([before, field, after], axis=1)
    even = lat % 2 == 0
    upper, lower = middle[:2], middle[-2:]
    from_inner = lax.ppermute(jnp.where(even, lower, upper), ("lat", "lon"), inner)
    from_outer = lax.ppermute(jnp.where(even, upper, lower), ("lat", "lon"), outer)
    above = jnp.where(even, from_outer, from_inner)
    below = jnp.where(even, from_inner, from_outer)
    north, south = lat == 0, lat == lats - 1
    top_window = jnp.where(
        north, jnp.concatenate([middle[:1], above]), jnp.concatenate([above, middle[:1]])
    )
    bottom_window = jnp.where(
        south, jnp.concatenate([below, middle[-1:]]), jnp.concatenate([middle[-1:], below])
    )
    row_above = jnp.where(north, above[:1], above[1:])
    row_below = jnp.where(south, below[1:], below[:1])
    stacked = jnp.concatenate([top_window, row_above, middle, row_below, bottom_window], axis=0)
    first = conv_valid(stacked, conv_first)
    hidden = jax.nn.silu((first + bias_first) * (1.0 + film_terms[0]) + film_terms[1]).astype(BF16)
    hidden = jnp.concatenate([hidden[:1], hidden[3 : 3 + height], hidden[-1:]], axis=0)
    second = conv_valid(hidden, conv_second)
    fine_out = (field.astype(F32) + second).astype(BF16)

    partial = kernel_call(
        attend_body, jax.ShapeDtypeStruct((n_xc, rows, 2 * heads_width), BF16)
    )(queries, pairs)
    partial = lax.all_to_all(partial, "lat", 0, 0, axis_index_groups=over_xc)
    projected = kernel_call(
        merge_body, jax.ShapeDtypeStruct((lons, rows, out_weight.shape[1] // lons), BF16)
    )(partial, out_weight)
    projected = lax.all_to_all(projected, "lon", 0, 0)
    bottleneck_out = kernel_call(finish_body, jax.ShapeDtypeStruct(tokens.shape, BF16))(projected, tokens)
    return (fine_out[None], bottleneck_out[None])


def solution(mesh):
    placed = (
        P(None, "lat", "lon", None),
        P(),
        P(),
        P(),
        P(),
        P(None, "lat", "lon"),
        P(None, "lon"),
        P(None, "lon"),
        P(None, "lon"),
        P("lon", None),
    )
    return jax.shard_map(
        shards,
        mesh=mesh,
        in_specs=placed,
        out_specs=(P(None, "lat", "lon", None), P(None, "lat", "lon")),
        check_vma=False,
    )
```

time: 325 us -> 115 us (0.35)
  the two profiles are of different devices: /device:TPU:1 before, /device:TPU:32 now
where the time goes in v1:
time: 115 us; the launch traced here: 114 us
  waiting for transfers between devices  44.5 us (39%)
  starting transfers between devices  43.3 us (38%)
  other arithmetic  10.7 us (9%)
  local copies, waits for them, and re-layouts  6.55 us (6%)
  Pallas kernels  4.46 us (4%)
  matrix products  3.7 us (3%)
    all_to_all x1, waiting for transfers between devices, shards(): incoming = lax.all_to_all(outgoing, 'lon', 0, 0)  18.9 us
    all_to_all x1, starting transfers between devices, shards(): incoming = lax.all_to_all(outgoing, 'lon', 0, 0)  16.8 us
    all_to_all x1, waiting for transfers between devices, shards(): projected = lax.all_to_all(projected, 'lon', 0, 0)  11.2 us
    all_to_all x1, starting transfers between devices, shards(): projected = lax.all_to_all(projected, 'lon', 0, 0)  7.43 us
    all_to_all x1, starting transfers between devices, shards(): pairs = lax.all_to_all(pairs, 'lat', 0, 0, axis_index_groups=over_z)  7.19 us
    all_to_all x1, waiting for transfers between devices, shards(): partial = lax.all_to_all(partial, 'lat', 0, 0, axis_index_groups=over_xc)  6.25 us
    all_to_all x1, waiting for transfers between devices, shards(): pairs = lax.all_to_all(pairs, 'lat', 0, 0, axis_index_groups=over_z)  5.34 us
    conv_general_dilated x10, local copies, waits for them, and re-layouts, conv_valid(): lax.conv_general_dilated(padded[None], kernel, (1, 1), 'VALID', dimension...  4.81 us
  transfers between devices with their start and end apart: 7, of which 5 were waited for; matrix products, arithmetic and copies ran while one was open for 15% of the time, Pallas kernels for 1%

profile of v1, /device:TPU:32, one launch (start us, length us, event | category | flops | bytes accessed | tf_op | source)
XLA Modules:
  0.0 114.1 jit_solution(17440560165623322286)
XLA Ops:
  0.6 0.0 copy-start
  0.7 0.8 fusion.33
  1.6 0.1 broadcast_select_fusion.4
  1.6 0.7 broadcast_in_dim.49
  2.4 0.7 pad_maximum_fusion.1
  3.0 16.8 %all-to-all-start = ((bf16[8,72,128]{2,1,0:T(8,128)(2,1)}), bf16[8,72,128]{2,1,0:T(8,128)(2,1)S(1)}, u32[]{:S(2)}, u32[]{:S(2)}) async-start(bf16[8,72,128]{2,1,0:T(8,128)(2,1)} %pad_maximum_fusion.1), calls=%async_computation | async-start | bytes 294912 | tf_op jit(solution)/shard_map/all_to_all | solution.py:150
  19.9 0.8 add_bitcast_fusion
  20.6 18.9 %all-to-all-done.tokens_ref = bf16[8,72,128]{2,1,0:T(8,128)(2,1)S(1)} async-done(((bf16[8,72,128]{2,1,0:T(8,128)(2,1)}), bf16[8,72,128]{2,1,0:T(8,128)(2,1)S(1)}, u32[]{:S(2)}, u32[]{:S(2)}) %all-to-all-start) | async-done | bytes 147488 | tf_op jit(solution)/shard_map/all_to_all | solution.py:150
  39.5 1.3 %pad_maximum_fusion = bf16[12,184,128]{2,1,0:T(8,128)(2,1)S(1)} fusion(bf16[12,2,128]{2,1,0:T(2,128)(2,1)S(1)} %bitcast.48, bf16[12,180,128]{2,1,0:T(8,128)(2,1)} %bitcast.44, bf16[12,2,128]{2,1,0:T(2,128)(2,1)S(1)} %bitcast.46), kind=kLoop, calls=%fused_computation.25 | loop fusion | flops 1695744 | bytes 1130496 | tf_op jit(solution)/shard_map/concatenate | solution.py:166
  40.8 1.9 %collective-permute-start.1 = (bf16[2,184,128]{2,1,0:T(8,128)(2,1)S(1)}, bf16[2,184,128]{2,1,0:T(8,128)(2,1)S(1)}, u32[]{:S(2)}, u32[]{:S(2)}) collective-permute-start(bf16[2,184,128]{2,1,0:T(8,128)(2,1)S(1)} %get-tuple-element.10), channel_id=1, source_target_pairs={{0,8},{1,9},{2,10},{3,11},{4,12},{5,13},{6,14},{7,15},{8,0},{9,1},... | collective-permute-start | bytes 282632 | tf_op jit(solution)/shard_map/ppermute | solution.py:169
  42.7 1.9 %collective-permute-start = (bf16[2,184,128]{2,1,0:T(8,128)(2,1)S(1)}, bf16[2,184,128]{2,1,0:T(8,128)(2,1)S(1)}, u32[]{:S(2)}, u32[]{:S(2)}) collective-permute-start(bf16[2,184,128]{2,1,0:T(8,128)(2,1)S(1)} %get-tuple-element.11), channel_id=1, source_target_pairs={{0,4},{1,5},{2,6},{3,7},{4,0},{5,1},{6,2},{7,3},{8,16},{9,17},{10,... | collective-permute-start | bytes 282632 | tf_op jit(solution)/shard_map/ppermute | solution.py:170
  44.7 1.0 shard_map.113
  45.7 4.4 %all-to-all-start.1 = ((bf16[8,48,128]{2,1,0:T(8,128)(2,1)}), bf16[8,48,128]{2,1,0:T(8,128)(2,1)S(1)}, u32[]{:S(2)}, u32[]{:S(2)}) async-start(bf16[8,48,128]{2,1,0:T(8,128)(2,1)} %get-tuple-element.4), calls=%async_computation.1 | async-start | bytes 196608 | tf_op jit(solution)/shard_map/all_to_all | solution.py:161
  50.1 0.0 collective-permute-done.1
  50.1 0.0 collective-permute-done
  50.2 0.7 fusion.21
  50.9 0.6 fusion.24
  51.5 1.0 constant_dynamic-update-slice_fusion
  52.5 0.6 fusion.23
  53.1 2.8 %all-to-all-done.1.q_ref = bf16[8,48,128]{2,1,0:T(8,128)(2,1)S(1)} async-done(((bf16[8,48,128]{2,1,0:T(8,128)(2,1)}), bf16[8,48,128]{2,1,0:T(8,128)(2,1)S(1)}, u32[]{:S(2)}, u32[]{:S(2)}) %all-to-all-start.1) | async-done | bytes 98336 | tf_op jit(solution)/shard_map/all_to_all | solution.py:161
  55.9 7.2 %all-to-all-start.2 = ((bf16[8,48,256]{2,1,0:T(8,128)(2,1)}), bf16[8,48,256]{2,1,0:T(8,128)(2,1)S(1)}, u32[]{:S(2)}, u32[]{:S(2)}) async-start(bf16[8,48,256]{2,1,0:T(8,128)(2,1)} %get-tuple-element.5), calls=%async_computation.2 | async-start | bytes 393216 | tf_op jit(solution)/shard_map/all_to_all | solution.py:162
  63.1 0.7 fusion.22
  63.8 1.4 %reshape.36 = bf16[20,1,8,23,128]{4,3,2,0,1:T(8,128)(2,1)S(1)} reshape(bf16[20,184,128]{2,1,0:T(8,128)(2,1)} %fusion.22) | data formatting | bytes 1884160 | tf_op jit(solution)/shard_map/conv_general_dilated | solution.py:115
  65.2 0.1 copy.13
  65.4 2.2 %convolution_select_fusion = f32[18,8,23,128]{3,1,2,0:T(8,128)S(1)} fusion(bf16[3,3,128,128]{3,2,1,0:T(8,128)(2,1)S(1)} %copy-done, bf16[20,1,7,2,128]{4,2,3,0,1:T(8,128)(2,1)S(1)} %slice.86, bf16[20,1,8,23,128]{4,2,3,0,1:T(8,128)(2,1)S(1)} %copy.13, pred[8,23]{0,1:T(8,128)(4,1)S(1)} %copy-done.10), kind=kOutput, calls=%fused_computation.9 | convolution fusion | flops 980244480 | bytes 3004600 | tf_op jit(solution)/shard_map/conv_general_dilated | solution.py:115
  67.6 0.3 copy.14
  67.9 0.0 copy-start.7
  67.9 1.3 %reshape.40 = f32[18,1,184,128]{3,2,0,1:T(8,128)} reshape(f32[18,8,23,128]{3,2,1,0:T(8,128)S(1)} %copy.14) | data formatting | bytes 3391488 | tf_op jit(solution)/shard_map/conv_general_dilated | solution.py:115
  69.3 2.0 %multiply_convert_fusion = bf16[18,182,128]{2,1,0:T(8,128)(2,1)S(1)} fusion(f32[18,1,184,128]{3,2,0,1:T(8,128)} %reshape.40, f32[128]{0:T(128)S(1)} %get-tuple-element.19, f32[128]{0:T(128)S(1)} %get-tuple-element.18, f32[128]{0:T(128)S(1)} %copy-done.7), kind=kLoop, calls=%fused_computation.6 | loop fusion | flops 3354624 | bytes 2517504 | tf_op jit(solution)/shard_map/convert_element_type | solution.py:184
  71.2 5.3 %all-to-all-done.2.kv_ref = bf16[8,48,256]{2,1,0:T(8,128)(2,1)S(1)} async-done(((bf16[8,48,256]{2,1,0:T(8,128)(2,1)}), bf16[8,48,256]{2,1,0:T(8,128)(2,1)S(1)}, u32[]{:S(2)}, u32[]{:S(2)}) %all-to-all-start.2) | async-done | bytes 196640 | tf_op jit(solution)/shard_map/all_to_all | solution.py:162
  76.6 1.7 %shard_map.114 = bf16[8,48,256]{2,1,0:T(8,128)(2,1)} custom-call(bf16[8,48,128]{2,1,0:T(8,128)(2,1)S(1)} %all-to-all-done.1.q_ref, bf16[8,48,256]{2,1,0:T(8,128)(2,1)S(1)} %all-to-all-done.2.kv_ref), custom_call_target="tpu_custom_call" | custom-call | tf_op jit(solution)/shard_map/pallas_call | solution.py:189
  78.3 3.6 %all-to-all-start.3 = ((bf16[8,48,256]{2,1,0:T(8,128)(2,1)}), bf16[8,48,256]{2,1,0:T(8,128)(2,1)S(1)}, u32[]{:S(2)}, u32[]{:S(2)}) async-start(bf16[8,48,256]{2,1,0:T(8,128)(2,1)} %shard_map.114), calls=%async_computation.3 | async-start | bytes 393216 | tf_op jit(solution)/shard_map/all_to_all | solution.py:192
  82.0 0.1 maximum_bitcast_fusion
  82.1 0.1 pad.1
  82.1 0.0 copy-start.4
  82.1 0.0 copy-start.8
  82.1 0.0 copy-start.9
  82.2 0.2 reshape.43
  82.4 0.1 copy.16
  82.5 6.3 %all-to-all-done.3.o_ref = bf16[8,48,256]{2,1,0:T(8,128)(2,1)S(1)} async-done(((bf16[8,48,256]{2,1,0:T(8,128)(2,1)}), bf16[8,48,256]{2,1,0:T(8,128)(2,1)S(1)}, u32[]{:S(2)}, u32[]{:S(2)}) %all-to-all-start.3) | async-done | bytes 196640 | tf_op jit(solution)/shard_map/all_to_all | solution.py:192
  88.7 1.1 shard_map.115
  89.9 7.4 %all-to-all-start.4 = ((bf16[8,48,128]{2,1,0:T(8,128)(2,1)}), bf16[8,48,128]{2,1,0:T(8,128)(2,1)S(1)}, u32[]{:S(2)}, u32[]{:S(2)}) async-start(bf16[8,48,128]{2,1,0:T(8,128)(2,1)} %shard_map.115), calls=%async_computation.4 | async-start | bytes 196608 | tf_op jit(solution)/shard_map/all_to_all | solution.py:196
  97.3 1.5 %convolution_select_fusion.1 = f32[12,8,23,128]{3,1,2,0:T(8,128)S(1)} fusion(bf16[3,3,128,128]{3,2,1,0:T(8,128)(2,1)S(1)} %copy-done.8, bf16[14,1,7,2,128]{4,2,3,0,1:T(8,128)(2,1)S(1)} %slice.91, bf16[14,1,8,23,128]{4,2,3,0,1:T(8,128)(2,1)S(1)} %copy.16, pred[8,23]{0,1:T(8,128)(4,1)S(1)} %copy-done.9), kind=kOutput, calls=%fused_computation.10 | convolution fusion | flops 653598720 | bytes 2135224 | tf_op jit(solution)/shard_map/conv_general_dilated | solution.py:115
  98.8 0.2 copy.17
  99.0 1.1 reshape.47
  100.1 2.2 %fusion.6 = bf16[1,12,180,128]{3,2,1,0:T(8,128)(2,1)} fusion(f32[12,1,184,128]{3,2,0,1:T(8,128)} %reshape.47, bf16[1,12,180,128]{3,2,1,0:T(8,128)(2,1)S(1)} %copy-done.6), kind=kLoop, calls=%fused_computation.13 | loop fusion | flops 829440 | bytes 2211840 | tf_op jit(solution)/shard_map/convert_element_type | solution.py:187
  102.3 11.2 %all-to-all-done.4.parts_ref = bf16[8,48,128]{2,1,0:T(8,128)(2,1)S(1)} async-done(((bf16[8,48,128]{2,1,0:T(8,128)(2,1)}), bf16[8,48,128]{2,1,0:T(8,128)(2,1)S(1)}, u32[]{:S(2)}, u32[]{:S(2)}) %all-to-all-start.4) | async-done | bytes 98336 | tf_op jit(solution)/shard_map/all_to_all | solution.py:196
  113.5 0.6 shard_map.116
  (26 shorter events, 0.2 us)
Async XLA Ops:
  0.6 64.8 %copy-start = (bf16[3,3,128,128]{3,2,1,0:T(8,128)(2,1)S(1)}, bf16[3,3,128,128]{3,2,1,0:T(8,128)(2,1)}, u32[]{:S(2)}) copy-start(bf16[3,3,128,128]{3,2,1,0:T(8,128)(2,1)} %param.11) | copy-start | bytes 884740
  0.6 44.0 %copy-start.3 = (bf16[1024,128]{1,0:T(8,128)(2,1)S(1)}, bf16[1024,128]{1,0:T(8,128)(2,1)}, u32[]{:S(2)}) copy-start(bf16[1024,128]{1,0:T(8,128)(2,1)} %wv_ref.1) | copy-start | bytes 786436
  0.7 44.0 %copy-start.2 = (bf16[1024,128]{1,0:T(8,128)(2,1)S(1)}, bf16[1024,128]{1,0:T(8,128)(2,1)}, u32[]{:S(2)}) copy-start(bf16[1024,128]{1,0:T(8,128)(2,1)} %wk_ref.1) | copy-start | bytes 786436
  0.7 44.0 %copy-start.1 = (bf16[1024,128]{1,0:T(8,128)(2,1)S(1)}, bf16[1024,128]{1,0:T(8,128)(2,1)}, u32[]{:S(2)}) copy-start(bf16[1024,128]{1,0:T(8,128)(2,1)} %wq_ref.1) | copy-start | bytes 786436
  3.0 36.4 %all-to-all-start = ((bf16[8,72,128]{2,1,0:T(8,128)(2,1)}), bf16[8,72,128]{2,1,0:T(8,128)(2,1)S(1)}, u32[]{:S(2)}, u32[]{:S(2)}) async-start(bf16[8,72,128]{2,1,0:T(8,128)(2,1)} %pad_maximum_fusion.1), calls=%async_computation | async-start | bytes 294912 | tf_op jit(solution)/shard_map/all_to_all | solution.py:150
  39.5 12.0 %copy-start.6 = (bf16[1,12,180,128]{3,2,1,0:T(8,128)(2,1)S(1)}, bf16[1,12,180,128]{3,2,1,0:T(8,128)(2,1)}, u32[]{:S(2)}) copy-start(bf16[1,12,180,128]{3,2,1,0:T(8,128)(2,1)} %param.10) | copy-start | bytes 1658884
  40.8 9.3 %collective-permute-start.1 = (bf16[2,184,128]{2,1,0:T(8,128)(2,1)S(1)}, bf16[2,184,128]{2,1,0:T(8,128)(2,1)S(1)}, u32[]{:S(2)}, u32[]{:S(2)}) collective-permute-start(bf16[2,184,128]{2,1,0:T(8,128)(2,1)S(1)} %get-tuple-element.10), channel_id=1, source_target_pairs={{0,8},{1,9},{2,10},{3,11},{4,12},{5,13},{6,14},{7,15},{8,0},{9,1},... | collective-permute-start | bytes 282632 | tf_op jit(solution)/shard_map/ppermute | solution.py:169
  42.7 7.4 %collective-permute-start = (bf16[2,184,128]{2,1,0:T(8,128)(2,1)S(1)}, bf16[2,184,128]{2,1,0:T(8,128)(2,1)S(1)}, u32[]{:S(2)}, u32[]{:S(2)}) collective-permute-start(bf16[2,184,128]{2,1,0:T(8,128)(2,1)S(1)} %get-tuple-element.11), channel_id=1, source_target_pairs={{0,4},{1,5},{2,6},{3,7},{4,0},{5,1},{6,2},{7,3},{8,16},{9,17},{10,... | collective-permute-start | bytes 282632 | tf_op jit(solution)/shard_map/ppermute | solution.py:170
  45.7 10.2 %all-to-all-start.1 = ((bf16[8,48,128]{2,1,0:T(8,128)(2,1)}), bf16[8,48,128]{2,1,0:T(8,128)(2,1)S(1)}, u32[]{:S(2)}, u32[]{:S(2)}) async-start(bf16[8,48,128]{2,1,0:T(8,128)(2,1)} %get-tuple-element.4), calls=%async_computation.1 | async-start | bytes 196608 | tf_op jit(solution)/shard_map/all_to_all | solution.py:161
  55.9 20.6 %all-to-all-start.2 = ((bf16[8,48,256]{2,1,0:T(8,128)(2,1)}), bf16[8,48,256]{2,1,0:T(8,128)(2,1)S(1)}, u32[]{:S(2)}, u32[]{:S(2)}) async-start(bf16[8,48,256]{2,1,0:T(8,128)(2,1)} %get-tuple-element.5), calls=%async_computation.2 | async-start | bytes 393216 | tf_op jit(solution)/shard_map/all_to_all | solution.py:162
  63.8 1.6 %copy-start.10 = (pred[8,23]{0,1:T(8,128)(4,1)S(1)}, pred[8,23]{0,1:T(8,128)(4,1)}, u32[]{:S(2)}) copy-start(pred[8,23]{0,1:T(8,128)(4,1)} %constant.64) | copy-start | bytes 556
  67.9 1.3 %copy-start.7 = (f32[128]{0:T(128)S(1)}, f32[128]{0:T(128)}, u32[]{:S(2)}) copy-start(f32[128]{0:T(128)} %param.12) | copy-start | bytes 1540
  78.3 10.5 %all-to-all-start.3 = ((bf16[8,48,256]{2,1,0:T(8,128)(2,1)}), bf16[8,48,256]{2,1,0:T(8,128)(2,1)S(1)}, u32[]{:S(2)}, u32[]{:S(2)}) async-start(bf16[8,48,256]{2,1,0:T(8,128)(2,1)} %shard_map.114), calls=%async_computation.3 | async-start | bytes 393216 | tf_op jit(solution)/shard_map/all_to_all | solution.py:192
  82.1 6.6 %copy-start.4 = (bf16[128,1024]{1,0:T(8,128)(2,1)S(1)}, bf16[128,1024]{1,0:T(8,128)(2,1)}, u32[]{:S(2)}) copy-start(bf16[128,1024]{1,0:T(8,128)(2,1)} %wo_ref.1) | copy-start | bytes 786436
  82.1 15.2 %copy-start.8 = (bf16[3,3,128,128]{3,2,1,0:T(8,128)(2,1)S(1)}, bf16[3,3,128,128]{3,2,1,0:T(8,128)(2,1)}, u32[]{:S(2)}) copy-start(bf16[3,3,128,128]{3,2,1,0:T(8,128)(2,1)} %param.14) | copy-start | bytes 884740
  82.1 15.2 %copy-start.9 = (pred[8,23]{0,1:T(8,128)(4,1)S(1)}, pred[8,23]{0,1:T(8,128)(4,1)}, u32[]{:S(2)}) copy-start(pred[8,23]{0,1:T(8,128)(4,1)} %constant.63) | copy-start | bytes 556
  89.9 23.6 %all-to-all-start.4 = ((bf16[8,48,128]{2,1,0:T(8,128)(2,1)}), bf16[8,48,128]{2,1,0:T(8,128)(2,1)S(1)}, u32[]{:S(2)}, u32[]{:S(2)}) async-start(bf16[8,48,128]{2,1,0:T(8,128)(2,1)} %shard_map.115), calls=%async_computation.4 | async-start | bytes 196608 | tf_op jit(solution)/shard_map/all_to_all | solution.py:196
  100.1 13.4 %copy-start.5 = (bf16[1,48,128]{2,1,0:T(8,128)(2,1)S(1)}, bf16[1,48,128]{2,1,0:T(8,128)(2,1)}, u32[]{:S(2)}) copy-start(bf16[1,48,128]{2,1,0:T(8,128)(2,1)} %param.15) | copy-start | bytes 36868

commit v2 on v1

v2 whole, which is shorter than its diff:
```python
import functools

import jax
import jax.numpy as jnp
from jax import lax
from jax.experimental import pallas as pl
from jax.experimental.pallas import tpu as pltpu
from jax.sharding import PartitionSpec as P

HEAD = 64
BF16 = jnp.bfloat16
F32 = jnp.float32
VMEM_LIMIT = 48 * 1024 * 1024


def lat_groups():
    place = lambda x, z, c: x * 16 + z * 2 + c
    over_z = [[place(x, z, c) for z in range(8)] for x in range(4) for c in range(2)]
    over_xc = [[place(x, z, c) for x in range(4) for c in range(2)] for z in range(8)]
    return over_z, over_xc


def halo_pairs(lat, lon):
    inner, outer = [], []
    for i in range(lat):
        for j in range(lon):
            me = i * lon + j
            inner.append((me, (i ^ 1) * lon + j))
            if i in (0, lat - 1):
                outer.append((me, i * lon + (j + lon // 2) % lon))
            else:
                outer.append((me, (i + 1 if i % 2 else i - 1) * lon + j))
    return inner, outer


def kernel_call(body, out_shape, **extra):
    return pl.pallas_call(
        body,
        out_shape=out_shape,
        compiler_params=pltpu.CompilerParams(vmem_limit_bytes=VMEM_LIMIT),
        **extra,
    )


def project_body(tokens_ref, weight_ref, q_ref, kv_ref):
    wide = jnp.concatenate([tokens_ref[j] for j in range(tokens_ref.shape[0])], axis=1).astype(F32)
    normed = (wide * lax.rsqrt(jnp.mean(wide * wide, axis=-1, keepdims=True) + 1e-06)).astype(BF16)
    q_width = q_ref.shape[1]
    flat = jnp.dot(normed, weight_ref[...], preferred_element_type=F32).astype(BF16)
    q_ref[...] = flat[:, :q_width]
    kv = flat[:, q_width:]
    for j in range(kv_ref.shape[0]):
        kv_ref[j] = kv


def attend_body(place_ref, q0_ref, q1_ref, q2_ref, q3_ref, kv_ref, o_ref):
    sources = (q0_ref, q1_ref, q2_ref, q3_ref)
    cores, rows, width = q0_ref.shape
    n = cores * len(sources)
    q = jnp.concatenate([ref[t] for ref in sources for t in range(cores)], axis=0)
    kv = kv_ref[...].reshape(kv_ref.shape[0] * kv_ref.shape[1], 2 * width)
    scale = 1.0 / HEAD**0.5
    outs = []
    lane = lax.broadcasted_iota(jnp.int32, (n * rows, width), 1)
    tail = jnp.zeros((n * rows, width), F32)
    for h in range(width // HEAD):
        qh = q[:, h * HEAD : (h + 1) * HEAD]
        kh = kv[:, h * HEAD : (h + 1) * HEAD]
        vh = kv[:, width + h * HEAD : width + (h + 1) * HEAD]
        scores = lax.dot_general(qh, kh, (((1,), (1,)), ((), ())), preferred_element_type=F32) * scale
        top = jnp.max(scores, axis=-1, keepdims=True)
        expo = jnp.exp(scores - top)
        total = jnp.sum(expo, axis=-1, keepdims=True)
        outs.append(jnp.dot(expo.astype(BF16), vh, preferred_element_type=F32) / total)
        rest = top + jnp.log(total)
        for part in range(3):
            piece = rest.astype(BF16).astype(F32)
            rest = rest - piece
            tail = jnp.where(lane == 3 * h + part, piece, tail)
    result = jnp.concatenate(outs + [tail], axis=1).astype(BF16)
    x, core = place_ref[0], place_ref[1]
    for s in range(len(sources)):
        for t in range(cores):
            at = lax.rem(x + s, len(sources)) * cores + (core if t == 0 else 1 - core)
            o_ref[at] = result[(s * cores + t) * rows : (s * cores + t + 1) * rows]


def merge_body(lon_ref, o_ref, wo_ref, first_ref, last_ref, out_ref):
    n, rows, width = o_ref.shape[0], o_ref.shape[1], o_ref.shape[2] // 2
    heads = []
    for h in range(width // HEAD):
        logs = []
        for p in range(n):
            pieces = o_ref[p, :, width : 2 * width].astype(F32)
            logs.append(pieces[:, 3 * h : 3 * h + 1] + pieces[:, 3 * h + 1 : 3 * h + 2] + pieces[:, 3 * h + 2 : 3 * h + 3])
        top = functools.reduce(jnp.maximum, logs)
        num = jnp.zeros((rows, HEAD), F32)
        total = jnp.zeros((rows, 1), F32)
        for p in range(n):
            weight = jnp.exp(logs[p] - top)
            total = total + weight
            num = num + weight * o_ref[p, :, h * HEAD : (h + 1) * HEAD].astype(F32)
        heads.append(num / total)
    attended = jnp.concatenate(heads, axis=1).astype(BF16)
    partial = jnp.dot(attended, wo_ref[...], preferred_element_type=F32).astype(BF16)
    lons = out_ref.shape[0]
    first, last = first_ref[...].astype(F32), last_ref[...].astype(F32)
    for j in range(lons):
        out_ref[j, :rows] = partial[:, j * width : (j + 1) * width]
        out_ref[j, rows:] = jnp.where(lax.rem(lon_ref[0] + 1, lons) == j, last, first).astype(BF16)


def three(row):
    return jnp.concatenate([pltpu.roll(row, 1, 0), row, pltpu.roll(row, row.shape[0] - 1, 0)], axis=1).astype(BF16)


def windows(wide_ref, above, rows, below, north, south):
    height = len(rows)
    wide_ref[0] = three(jnp.where(north, rows[0](), above[0]))
    wide_ref[1] = three(jnp.where(north, above[0], above[1]))
    wide_ref[2] = three(jnp.where(north, above[1], rows[0]()))
    wide_ref[3] = three(jnp.where(north, above[0], above[1]))
    for r in range(height):
        wide_ref[4 + r] = three(rows[r]())
    wide_ref[4 + height] = three(jnp.where(south, below[1], below[0]))
    wide_ref[5 + height] = three(jnp.where(south, below[0], rows[-1]()))
    wide_ref[6 + height] = three(jnp.where(south, below[1], below[0]))
    wide_ref[7 + height] = three(jnp.where(south, rows[-1](), below[1]))


def conv(source, start, count, kernel):
    _, ring, deep = source.shape
    total = None
    for dy in range(3):
        part = source[start + dy : start + dy + count].reshape(count * ring, deep)
        product = jnp.dot(part, kernel[dy], preferred_element_type=F32)
        total = product if total is None else total + product
    return total


def activate(first, bias_ref, film_ref):
    u = (first + bias_ref[...]) * (1.0 + film_ref[0:1]) + film_ref[1:2]
    return (u / (1.0 + jnp.exp(-u))).astype(BF16).astype(F32)


def conv_body(
    flags_ref, field_ref, inner_ref, outer_ref, first_ref, bias_ref, film_ref, second_ref, out_ref, wide_ref, hidden_ref
):
    height, width, channels = field_ref.shape
    ring = wide_ref.shape[1]
    north, south, even = (flags_ref[i] == 1 for i in range(3))
    gap = jnp.zeros((ring - width, channels), F32)

    def ringed(row):
        return jnp.concatenate([row.astype(F32), gap])

    def halo(i, yes_ref, no_ref):
        return ringed(jnp.where(even, yes_ref[i].astype(F32), no_ref[i].astype(F32)))

    above = [halo(i, outer_ref, inner_ref) for i in range(2)]
    below = [halo(i, inner_ref, outer_ref) for i in range(2)]
    rows = [lambda r=r: ringed(field_ref[r]) for r in range(height)]
    windows(wide_ref, above, rows, below, north, south)

    hidden_ref[0] = three(activate(conv(wide_ref, 0, 1, first_ref), bias_ref, film_ref))
    hidden_ref[height + 1] = three(activate(conv(wide_ref, height + 5, 1, first_ref), bias_ref, film_ref))
    block = 4
    for r in range(0, height, block):
        done = activate(conv(wide_ref, 3 + r, block, first_ref), bias_ref, film_ref)
        for i in range(block):
            hidden_ref[1 + r + i] = three(done[i * ring : (i + 1) * ring])
    for r in range(0, height, block):
        done = conv(hidden_ref, r, block, second_ref)
        for i in range(block):
            out_ref[r + i] = (field_ref[r + i].astype(F32) + done[i * ring : i * ring + width]).astype(BF16)


def finish_body(
    flags_ref,
    parts_ref,
    tokens_ref,
    main_ref,
    strip_ref,
    first_ref,
    bias_ref,
    film_ref,
    second_ref,
    tokens_out_ref,
    field_out_ref,
    wide_ref,
    hidden_ref,
):
    lons = parts_ref.shape[0]
    rows = tokens_ref.shape[0]
    height, width, _ = main_ref.shape
    ring = wide_ref.shape[1]
    north, south, lon = flags_ref[0] == 1, flags_ref[1] == 1, flags_ref[3]
    shared = parts_ref[0, :rows].astype(F32)
    for j in range(1, lons):
        shared = shared + parts_ref[j, :rows].astype(F32)
    tokens_out_ref[...] = (tokens_ref[...].astype(F32) + shared).astype(BF16)

    left = parts_ref[lax.rem(lon + lons - 1, lons), rows:].astype(F32)
    right = parts_ref[lax.rem(lon + 1, lons), rows:].astype(F32)
    tall = strip_ref.shape[0]

    def ringed(i):
        return jnp.concatenate(
            [strip_ref[i].astype(F32)] + [side[c * tall + i : c * tall + i + 1] for side in (right, left) for c in range(2)]
        )

    windows(
        wide_ref,
        [ringed(0), ringed(1)],
        [lambda r=r: ringed(2 + r) for r in range(height)],
        [ringed(tall - 2), ringed(tall - 1)],
        north,
        south,
    )
    done = activate(conv(wide_ref, 0, height + 6, first_ref), bias_ref, film_ref)
    for r in range(height + 2):
        at = 0 if r == 0 else height + 5 if r == height + 1 else r + 2
        hidden_ref[r] = three(done[at * ring : (at + 1) * ring])
    done = conv(hidden_ref, 0, height, second_ref)
    field_out_ref[...] = main_ref[...]
    lane = lax.broadcasted_iota(jnp.int32, (ring, done.shape[1]), 0)
    tail = width - width // ring * ring
    side = strip_ref.shape[1] // 2
    for r in range(height):
        own = jnp.concatenate([strip_ref[r + 2].astype(F32), jnp.zeros((ring - 2 * side, done.shape[1]), F32)])
        made = own + done[r * ring : (r + 1) * ring]
        field_out_ref[r, :ring] = jnp.where(lane < 2, made, main_ref[r, :ring].astype(F32)).astype(BF16)
        end = made[2 * side - tail : 2 * side]
        field_out_ref[r, width - tail :] = jnp.where(
            lane[:tail] >= tail - 2, end, main_ref[r, width - tail :].astype(F32)
        ).astype(BF16)


def shards(
    fine_field,
    conv_first,
    bias_first,
    film_terms,
    conv_second,
    bottleneck_in,
    query_weight,
    key_weight,
    value_weight,
    out_weight,
):
    lats, lons = lax.axis_size("lat"), lax.axis_size("lon")
    lat, lon = lax.axis_index("lat"), lax.axis_index("lon")
    over_z, over_xc = lat_groups()
    inner, outer = halo_pairs(lats, lons)
    field, tokens = fine_field[0], bottleneck_in[0]
    height, width, channels = field.shape
    rows = tokens.shape[0]

    incoming = lax.all_to_all(jnp.broadcast_to(tokens[None], (lons,) + tokens.shape), "lon", 0, 0)

    even = lat % 2 == 0
    weights = jnp.concatenate([query_weight, key_weight, value_weight], axis=1)
    upper, lower, weights = lax.optimization_barrier((field[:2], field[-2:], weights))
    from_inner = lax.ppermute(jnp.where(even, lower, upper), ("lat", "lon"), inner)
    from_outer = lax.ppermute(jnp.where(even, upper, lower), ("lat", "lon"), outer)
    above = jnp.where(even, from_outer, from_inner)
    below = jnp.where(even, from_inner, from_outer)

    heads_width = query_weight.shape[1]
    n_z, n_xc = len(over_z[0]), len(over_xc[0])
    queries, pairs = kernel_call(
        project_body,
        (
            jax.ShapeDtypeStruct((rows, heads_width), BF16),
            jax.ShapeDtypeStruct((n_z, rows, 2 * heads_width), BF16),
        ),
    )(incoming, weights)
    pairs = lax.all_to_all(pairs, "lat", 0, 0, axis_index_groups=over_z)
    other = lax.ppermute(queries, "lat", [(i, i ^ 1) for i in range(lats)])
    chip = jnp.stack([queries, other])
    step = lats // 4
    gathered = [chip] + [
        lax.ppermute(chip, "lat", [(i, (i - s * step) % lats) for i in range(lats)]) for s in range(1, 4)
    ]

    place = jnp.stack([lat // step, lat % 2]).astype(jnp.int32)
    partial = pl.pallas_call(
        attend_body,
        in_specs=[pl.BlockSpec(memory_space=pltpu.SMEM)] + [pl.BlockSpec(memory_space=pltpu.VMEM)] * 5,
        out_shape=jax.ShapeDtypeStruct((n_xc, rows, 2 * heads_width), BF16),
        compiler_params=pltpu.CompilerParams(vmem_limit_bytes=VMEM_LIMIT),
    )(place, *gathered, pairs)

    partial = lax.all_to_all(partial, "lat", 0, 0, axis_index_groups=over_xc)
    side = 6
    ends = lambda rows: jnp.concatenate([rows[:, :side], rows[:, -side:]], axis=1)
    strip = jnp.concatenate([ends(above), ends(field), ends(below)])
    tall = height + 4
    first_columns = jnp.concatenate([strip[:, 0], strip[:, 1]])
    last_columns = jnp.concatenate([strip[:, -2], strip[:, -1]])
    smem, vmem = pl.BlockSpec(memory_space=pltpu.SMEM), pl.BlockSpec(memory_space=pltpu.VMEM)
    params = pltpu.CompilerParams(vmem_limit_bytes=VMEM_LIMIT)
    projected = pl.pallas_call(
        merge_body,
        in_specs=[smem] + [vmem] * 4,
        out_shape=jax.ShapeDtypeStruct((lons, rows + 2 * tall, out_weight.shape[1] // lons), BF16),
        compiler_params=params,
    )(lon.reshape(1).astype(jnp.int32), partial, out_weight, first_columns, last_columns)
    projected = lax.all_to_all(projected, "lon", 0, 0)

    flags = jnp.stack([lat == 0, lat == lats - 1, even, lon]).astype(jnp.int32)
    kernels = (
        conv_first.reshape(3, 3 * channels, channels),
        bias_first.reshape(1, channels),
        film_terms,
        conv_second.reshape(3, 3 * channels, channels),
    )
    ring = -(-width // 16) * 16
    main = pl.pallas_call(
        conv_body,
        in_specs=[smem] + [vmem] * 7,
        out_shape=jax.ShapeDtypeStruct(field.shape, BF16),
        scratch_shapes=[
            pltpu.VMEM((height + 8, ring, 3 * channels), BF16),
            pltpu.VMEM((height + 2, ring, 3 * channels), BF16),
        ],
        compiler_params=params,
    )(flags, field, from_inner, from_outer, *kernels)
    bottleneck_out, fine_out = pl.pallas_call(
        finish_body,
        in_specs=[smem] + [vmem] * 8,
        out_shape=(jax.ShapeDtypeStruct(tokens.shape, BF16), jax.ShapeDtypeStruct(field.shape, BF16)),
        scratch_shapes=[
            pltpu.VMEM((height + 8, 2 * side + 4, 3 * channels), BF16),
            pltpu.VMEM((height + 2, 2 * side + 4, 3 * channels), BF16),
        ],
        compiler_params=params,
    )(flags, projected, tokens, main, strip, *kernels)
    return (fine_out[None], bottleneck_out[None])


def solution(mesh):
    placed = (
        P(None, "lat", "lon", None),
        P(),
        P(),
        P(),
        P(),
        P(None, "lat", "lon"),
        P(None, "lon"),
        P(None, "lon"),
        P(None, "lon"),
        P("lon", None),
    )
    return jax.shard_map(
        shards,
        mesh=mesh,
        in_specs=placed,
        out_specs=(P(None, "lat", "lon", None), P(None, "lat", "lon")),
        check_vma=False,
    )
```

time: 115 us -> 103 us (0.90)
  the two profiles are of different devices: /device:TPU:32 before, /device:TPU:192 now
where the time goes in v2:
time: 103 us; the launch traced here: 102 us
  starting transfers between devices  53.5 us (52%)
  waiting for transfers between devices  33.3 us (32%)
  Pallas kernels  10.6 us (10%)
  local copies, waits for them, and re-layouts  2.48 us (2%)
  other arithmetic  1.36 us (1%)
    all_to_all x1, waiting for transfers between devices, shards(): projected = lax.all_to_all(projected, 'lon', 0, 0)  14.7 us
    ppermute x3, starting transfers between devices, shards(): lax.ppermute(chip, 'lat', [(i, (i - s * step) % lats) for i in range(lats)])  11.4 us
    all_to_all x1, starting transfers between devices, shards(): lax.all_to_all(jnp.broadcast_to(tokens[None], (lons,) + tokens.shape), 'l...  11.1 us
    all_to_all x1, starting transfers between devices, shards(): projected = lax.all_to_all(projected, 'lon', 0, 0)  10.9 us
    all_to_all x1, starting transfers between devices, shards(): pairs = lax.all_to_all(pairs, 'lat', 0, 0, axis_index_groups=over_z)  9.38 us
    all_to_all x1, waiting for transfers between devices, shards(): lax.all_to_all(jnp.broadcast_to(tokens[None], (lons,) + tokens.shape), 'l...  8.01 us
    all_to_all x1, waiting for transfers between devices, shards(): partial = lax.all_to_all(partial, 'lat', 0, 0, axis_index_groups=over_xc)  6.73 us
    pallas_call x1, Pallas kernels, shards(): pl.pallas_call(conv_body, in_specs=[smem] + [vmem] * 7, out_shape=jax.Sha...  4.26 us
  transfers between devices with their start and end apart: 10, of which 5 were waited for; matrix products, arithmetic and copies ran while one was open for 2% of the time, Pallas kernels for 5%

profile of v2, /device:TPU:192, one launch (start us, length us, event | category | flops | bytes accessed | tf_op | source)
XLA Modules:
  0.0 102.2 jit_solution(14907988703509561447)
XLA Ops:
  0.6 0.0 copy-start.7
  0.6 0.0 copy-start.8
  0.6 1.4 %broadcast_in_dim.14 = bf16[8,48,128]{2,1,0:T(8,128)(2,1)} broadcast(bf16[48,128]{1,0:T(8,128)(2,1)} %bitcast.37), dimensions={1,2} | broadcast | bytes 110592 | tf_op jit(solution)/shard_map/broadcast_in_dim | solution.py:259
  2.1 11.1 %all-to-all-start = ((bf16[8,48,128]{2,1,0:T(8,128)(2,1)}), bf16[8,48,128]{2,1,0:T(8,128)(2,1)S(1)}, u32[]{:S(2)}, u32[]{:S(2)}) async-start(bf16[8,48,128]{2,1,0:T(8,128)(2,1)} %broadcast_in_dim.14), calls=%async_computation | async-start | bytes 196608 | tf_op jit(solution)/shard_map/all_to_all | solution.py:259
  13.2 1.0 slice_bitcast_fusion
  14.1 0.0 copy-done.7
  14.1 0.0 copy-done.8
  14.2 0.0 copy-start.2
  14.2 1.1 %pad_maximum_fusion.weight_ref = bf16[1024,384]{1,0:T(8,128)(2,1)S(1)} fusion(bf16[1024,128]{1,0:T(8,128)(2,1)S(1)} %copy-done.7, bf16[1024,128]{1,0:T(8,128)(2,1)S(1)} %copy-done.8, bf16[1024,128]{1,0:T(8,128)(2,1)} %param.16), kind=kLoop, calls=%fused_computation | loop fusion | flops 2359296 | bytes 1572864 | tf_op jit(solution)/shard_map/concatenate | solution.py:262
  15.3 2.1 %collective-permute-start.4 = (bf16[2,180,128]{2,1,0:T(8,128)(2,1)S(1)}, bf16[2,180,128]{2,1,0:T(8,128)(2,1)S(1)}, u32[]{:S(2)}, u32[]{:S(2)}) collective-permute-start(bf16[2,180,128]{2,1,0:T(8,128)(2,1)S(1)} %get-tuple-element.22), channel_id=1, source_target_pairs={{0,4},{1,5},{2,6},{3,7},{4,0},{5,1},{6,2},{7,3},{8,16},{9,17},{10,... | collective-permute-start | bytes 276488 | tf_op jit(solution)/shard_map/ppermute | solution.py:265
  17.4 2.9 %collective-permute-start.5 = (bf16[2,180,128]{2,1,0:T(8,128)(2,1)S(1)}, bf16[2,180,128]{2,1,0:T(8,128)(2,1)S(1)}, u32[]{:S(2)}, u32[]{:S(2)}) collective-permute-start(bf16[2,180,128]{2,1,0:T(8,128)(2,1)S(1)} %get-tuple-element.23), channel_id=1, source_target_pairs={{0,8},{1,9},{2,10},{3,11},{4,12},{5,13},{6,14},{7,15},{8,0},{9,1},... | collective-permute-start | bytes 276488 | tf_op jit(solution)/shard_map/ppermute | solution.py:264
  20.3 0.0 copy-done.2
  20.3 0.1 pad_add_fusion.1.place_ref
  20.4 8.0 %all-to-all-done.tokens_ref = bf16[8,48,128]{2,1,0:T(8,128)(2,1)S(1)} async-done(((bf16[8,48,128]{2,1,0:T(8,128)(2,1)}), bf16[8,48,128]{2,1,0:T(8,128)(2,1)S(1)}, u32[]{:S(2)}, u32[]{:S(2)}) %all-to-all-start) | async-done | bytes 98336 | tf_op jit(solution)/shard_map/all_to_all | solution.py:259
  28.4 1.0 shard_map.113
  29.4 9.4 %all-to-all-start.1 = ((bf16[8,48,256]{2,1,0:T(8,128)(2,1)}), bf16[8,48,256]{2,1,0:T(8,128)(2,1)S(1)}, u32[]{:S(2)}, u32[]{:S(2)}) async-start(bf16[8,48,256]{2,1,0:T(8,128)(2,1)} %get-tuple-element.11), calls=%async_computation.1 | async-start | bytes 393216 | tf_op jit(solution)/shard_map/all_to_all | solution.py:278
  38.8 0.0 copy-start.3
  38.8 0.0 collective-permute-done.4.outer_ref
  38.8 0.0 collective-permute-done.5.inner_ref
  38.8 2.3 %collective-permute-start = (bf16[48,128]{1,0:T(8,128)(2,1)S(1)}, bf16[48,128]{1,0:T(8,128)(2,1)S(1)}, u32[]{:S(2)}, u32[]{:S(2)}) collective-permute-start(bf16[48,128]{1,0:T(8,128)(2,1)S(1)} %get-tuple-element.10), channel_id=1, source_target_pairs={{0,8},{8,0},{16,24},{24,16},{32,40},{40,32},{48,56},{56,48},{64,72... | collective-permute-start | bytes 36872 | tf_op jit(solution)/shard_map/ppermute | solution.py:279
  41.1 0.9 collective-permute-done
  42.1 3.4 %collective-permute-start.3 = (bf16[2,48,128]{2,1,0:T(8,128)(2,1)S(1)}, bf16[2,48,128]{2,1,0:T(8,128)(2,1)S(1)}, u32[]{:S(2)}, u32[]{:S(2)}) collective-permute-start(bf16[2,48,128]{2,1,0:T(8,128)(2,1)S(1)} %pad_maximum_fusion.1.q0_ref), channel_id=1, source_target_pairs={{0,128},{8,136},{16,144},{24,152},{32,160},{40,168},{48,176},{56,1... | collective-permute-start | bytes 73736 | tf_op jit(solution)/shard_map/ppermute | solution.py:283
  45.4 5.3 %collective-permute-start.2 = (bf16[2,48,128]{2,1,0:T(8,128)(2,1)S(1)}, bf16[2,48,128]{2,1,0:T(8,128)(2,1)S(1)}, u32[]{:S(2)}, u32[]{:S(2)}) collective-permute-start(bf16[2,48,128]{2,1,0:T(8,128)(2,1)S(1)} %pad_maximum_fusion.1.q0_ref), channel_id=1, source_target_pairs={{0,256},{8,264},{16,272},{24,280},{32,288},{40,296},{48,304},{56,3... | collective-permute-start | bytes 73736 | tf_op jit(solution)/shard_map/ppermute | solution.py:283
  50.8 2.7 %collective-permute-start.1 = (bf16[2,48,128]{2,1,0:T(8,128)(2,1)S(1)}, bf16[2,48,128]{2,1,0:T(8,128)(2,1)S(1)}, u32[]{:S(2)}, u32[]{:S(2)}) collective-permute-start(bf16[2,48,128]{2,1,0:T(8,128)(2,1)S(1)} %pad_maximum_fusion.1.q0_ref), channel_id=1, source_target_pairs={{0,384},{8,392},{16,400},{24,408},{32,416},{40,424},{48,432},{56,4... | collective-permute-start | bytes 73736 | tf_op jit(solution)/shard_map/ppermute | solution.py:283
  53.5 0.0 collective-permute-done.3.q3_ref
  53.5 0.0 collective-permute-done.2.q2_ref
  53.5 2.9 %collective-permute-done.1.q1_ref = bf16[2,48,128]{2,1,0:T(8,128)(2,1)S(1)} collective-permute-done((bf16[2,48,128]{2,1,0:T(8,128)(2,1)S(1)}, bf16[2,48,128]{2,1,0:T(8,128)(2,1)S(1)}, u32[]{:S(2)}, u32[]{:S(2)}) %collective-permute-start.1) | collective-permute-done | bytes 24608 | tf_op jit(solution)/shard_map/ppermute | solution.py:283
  56.5 0.0 all-to-all-done.1.kv_ref
  56.5 2.2 %shard_map.114 = bf16[8,48,256]{2,1,0:T(8,128)(2,1)} custom-call(s32[2]{0:T(128)S(1)} %pad_add_fusion.1.place_ref, bf16[2,48,128]{2,1,0:T(8,128)(2,1)S(1)} %pad_maximum_fusion.1.q0_ref, bf16[2,48,128]{2,1,0:T(8,128)(2,1)S(1)} %collective-permute-done.1.q1_ref, bf16[2,48,128]{2,1,0:T(8,128)(2,1)S(1)} %collective-permute-done.2.q2_ref, ...), custom_call_target="tpu_custom_call" | custom-call | tf_op jit(solution)/shard_map/pallas_call | solution.py:287
  58.7 0.0 copy-start
  58.7 0.0 copy-start.1
  58.7 0.0 copy-start.5
  58.7 0.0 copy-start.6
  58.7 3.5 %all-to-all-start.2 = ((bf16[8,48,256]{2,1,0:T(8,128)(2,1)}), bf16[8,48,256]{2,1,0:T(8,128)(2,1)S(1)}, u32[]{:S(2)}, u32[]{:S(2)}) async-start(bf16[8,48,256]{2,1,0:T(8,128)(2,1)} %shard_map.114), calls=%async_computation.2 | async-start | bytes 393216 | tf_op jit(solution)/shard_map/all_to_all | solution.py:294
  62.3 6.7 %all-to-all-done.2.o_ref = bf16[8,48,256]{2,1,0:T(8,128)(2,1)S(1)} async-done(((bf16[8,48,256]{2,1,0:T(8,128)(2,1)}), bf16[8,48,256]{2,1,0:T(8,128)(2,1)S(1)}, u32[]{:S(2)}, u32[]{:S(2)}) %all-to-all-start.2) | async-done | bytes 196640 | tf_op jit(solution)/shard_map/all_to_all | solution.py:294
  69.0 0.0 copy-done.3
  69.0 1.2 %shard_map.115 = bf16[8,80,128]{2,1,0:T(8,128)(2,1)} custom-call(s32[1]{0:T(128)} %bitcast.3.lon_ref, bf16[8,48,256]{2,1,0:T(8,128)(2,1)S(1)} %all-to-all-done.2.o_ref, bf16[128,1024]{1,0:T(8,128)(2,1)S(1)} %copy-done.3, bf16[32,128]{1,0:T(8,128)(2,1)S(1)} %pad_maximum_fusion.2.first_ref, bf16[32,128]{1,0:T(8,128)(2,1)S(1)} %pad_maximum_fusion.3.last_ref), custom_call_target="tpu_custom_call" | custom-call | tf_op jit(solution)/shard_map/pallas_call | solution.py:303
  70.2 10.9 %all-to-all-start.3 = ((bf16[8,80,128]{2,1,0:T(8,128)(2,1)}), bf16[8,80,128]{2,1,0:T(8,128)(2,1)S(1)}, u32[]{:S(2)}, u32[]{:S(2)}) async-start(bf16[8,80,128]{2,1,0:T(8,128)(2,1)} %shard_map.115), calls=%async_computation.3 | async-start | bytes 327680 | tf_op jit(solution)/shard_map/all_to_all | solution.py:309
  81.1 0.1 pad_add_fusion.flags_ref
  81.2 0.0 copy-done
  81.2 0.0 copy-done.1
  81.2 0.0 copy-done.5
  81.2 0.0 copy-done.6
  81.2 0.0 copy-start.4
  81.2 4.3 %shard_map.116.main_ref = bf16[12,180,128]{2,1,0:T(8,128)(2,1)S(1)} custom-call(s32[4]{0:T(128)S(1)} %pad_add_fusion.flags_ref, bf16[12,180,128]{2,1,0:T(8,128)(2,1)S(1)} %bitcast.36, bf16[2,180,128]{2,1,0:T(8,128)(2,1)S(1)} %collective-permute-done.5.inner_ref, bf16[2,180,128]{2,1,0:T(8,128)(2,1)S(1)} %collective-permute-done.4.outer_ref, ...), custom_call_target="tpu_custom_call" | custom-call | tf_op jit(solution)/shard_map/pallas_call | solution.py:319
  85.5 14.7 %all-to-all-done.3.parts_ref = bf16[8,80,128]{2,1,0:T(8,128)(2,1)S(1)} async-done(((bf16[8,80,128]{2,1,0:T(8,128)(2,1)}), bf16[8,80,128]{2,1,0:T(8,128)(2,1)S(1)}, u32[]{:S(2)}, u32[]{:S(2)}) %all-to-all-start.3) | async-done | bytes 163872 | tf_op jit(solution)/shard_map/all_to_all | solution.py:309
  100.2 0.0 copy-done.4
  100.2 2.0 %shard_map.117 = (bf16[48,128]{1,0:T(8,128)(2,1)}, bf16[12,180,128]{2,1,0:T(8,128)(2,1)}) custom-call(s32[4]{0:T(128)S(1)} %pad_add_fusion.flags_ref, bf16[8,80,128]{2,1,0:T(8,128)(2,1)S(1)} %all-to-all-done.3.parts_ref, bf16[48,128]{1,0:T(8,128)(2,1)S(1)} %bitcast.38, bf16[12,180,128]{2,1,0:T(8,128)(2,1)S(1)} %shard_map.116.main_ref, ...), custom_call_target="tpu_custom_call" | custom-call | tf_op jit(solution)/shard_map/pallas_call | solution.py:329
  (13 shorter events, 0.2 us)
Async XLA Ops:
  0.6 13.5 %copy-start.7 = (bf16[1024,128]{1,0:T(8,128)(2,1)S(1)}, bf16[1024,128]{1,0:T(8,128)(2,1)}, u32[]{:S(2)}) copy-start(bf16[1024,128]{1,0:T(8,128)(2,1)} %param.18) | copy-start | bytes 786436
  0.6 13.5 %copy-start.8 = (bf16[1024,128]{1,0:T(8,128)(2,1)S(1)}, bf16[1024,128]{1,0:T(8,128)(2,1)}, u32[]{:S(2)}) copy-start(bf16[1024,128]{1,0:T(8,128)(2,1)} %param.17) | copy-start | bytes 786436
  2.1 26.4 %all-to-all-start = ((bf16[8,48,128]{2,1,0:T(8,128)(2,1)}), bf16[8,48,128]{2,1,0:T(8,128)(2,1)S(1)}, u32[]{:S(2)}, u32[]{:S(2)}) async-start(bf16[8,48,128]{2,1,0:T(8,128)(2,1)} %broadcast_in_dim.14), calls=%async_computation | async-start | bytes 196608 | tf_op jit(solution)/shard_map/all_to_all | solution.py:259
  14.2 6.1 %copy-start.2 = (bf16[1,12,180,128]{3,2,1,0:T(8,128)(2,1)S(1)}, bf16[1,12,180,128]{3,2,1,0:T(8,128)(2,1)}, u32[]{:S(2)}) copy-start(bf16[1,12,180,128]{3,2,1,0:T(8,128)(2,1)} %param.10) | copy-start | bytes 1658884
  15.3 23.5 %collective-permute-start.4 = (bf16[2,180,128]{2,1,0:T(8,128)(2,1)S(1)}, bf16[2,180,128]{2,1,0:T(8,128)(2,1)S(1)}, u32[]{:S(2)}, u32[]{:S(2)}) collective-permute-start(bf16[2,180,128]{2,1,0:T(8,128)(2,1)S(1)} %get-tuple-element.22), channel_id=1, source_target_pairs={{0,4},{1,5},{2,6},{3,7},{4,0},{5,1},{6,2},{7,3},{8,16},{9,17},{10,... | collective-permute-start | bytes 276488 | tf_op jit(solution)/shard_map/ppermute | solution.py:265
  17.4 21.4 %collective-permute-start.5 = (bf16[2,180,128]{2,1,0:T(8,128)(2,1)S(1)}, bf16[2,180,128]{2,1,0:T(8,128)(2,1)S(1)}, u32[]{:S(2)}, u32[]{:S(2)}) collective-permute-start(bf16[2,180,128]{2,1,0:T(8,128)(2,1)S(1)} %get-tuple-element.23), channel_id=1, source_target_pairs={{0,8},{1,9},{2,10},{3,11},{4,12},{5,13},{6,14},{7,15},{8,0},{9,1},... | collective-permute-start | bytes 276488 | tf_op jit(solution)/shard_map/ppermute | solution.py:264
  29.4 27.1 %all-to-all-start.1 = ((bf16[8,48,256]{2,1,0:T(8,128)(2,1)}), bf16[8,48,256]{2,1,0:T(8,128)(2,1)S(1)}, u32[]{:S(2)}, u32[]{:S(2)}) async-start(bf16[8,48,256]{2,1,0:T(8,128)(2,1)} %get-tuple-element.11), calls=%async_computation.1 | async-start | bytes 393216 | tf_op jit(solution)/shard_map/all_to_all | solution.py:278
  38.8 30.3 %copy-start.3 = (bf16[128,1024]{1,0:T(8,128)(2,1)S(1)}, bf16[128,1024]{1,0:T(8,128)(2,1)}, u32[]{:S(2)}) copy-start(bf16[128,1024]{1,0:T(8,128)(2,1)} %wo_ref.1) | copy-start | bytes 786436
  38.8 3.2 %collective-permute-start = (bf16[48,128]{1,0:T(8,128)(2,1)S(1)}, bf16[48,128]{1,0:T(8,128)(2,1)S(1)}, u32[]{:S(2)}, u32[]{:S(2)}) collective-permute-start(bf16[48,128]{1,0:T(8,128)(2,1)S(1)} %get-tuple-element.10), channel_id=1, source_target_pairs={{0,8},{8,0},{16,24},{24,16},{32,40},{40,32},{48,56},{56,48},{64,72... | collective-permute-start | bytes 36872 | tf_op jit(solution)/shard_map/ppermute | solution.py:279
  42.1 11.5 %collective-permute-start.3 = (bf16[2,48,128]{2,1,0:T(8,128)(2,1)S(1)}, bf16[2,48,128]{2,1,0:T(8,128)(2,1)S(1)}, u32[]{:S(2)}, u32[]{:S(2)}) collective-permute-start(bf16[2,48,128]{2,1,0:T(8,128)(2,1)S(1)} %pad_maximum_fusion.1.q0_ref), channel_id=1, source_target_pairs={{0,128},{8,136},{16,144},{24,152},{32,160},{40,168},{48,176},{56,1... | collective-permute-start | bytes 73736 | tf_op jit(solution)/shard_map/ppermute | solution.py:283
  45.4 8.1 %collective-permute-start.2 = (bf16[2,48,128]{2,1,0:T(8,128)(2,1)S(1)}, bf16[2,48,128]{2,1,0:T(8,128)(2,1)S(1)}, u32[]{:S(2)}, u32[]{:S(2)}) collective-permute-start(bf16[2,48,128]{2,1,0:T(8,128)(2,1)S(1)} %pad_maximum_fusion.1.q0_ref), channel_id=1, source_target_pairs={{0,256},{8,264},{16,272},{24,280},{32,288},{40,296},{48,304},{56,3... | collective-permute-start | bytes 73736 | tf_op jit(solution)/shard_map/ppermute | solution.py:283
  50.8 5.7 %collective-permute-start.1 = (bf16[2,48,128]{2,1,0:T(8,128)(2,1)S(1)}, bf16[2,48,128]{2,1,0:T(8,128)(2,1)S(1)}, u32[]{:S(2)}, u32[]{:S(2)}) collective-permute-start(bf16[2,48,128]{2,1,0:T(8,128)(2,1)S(1)} %pad_maximum_fusion.1.q0_ref), channel_id=1, source_target_pairs={{0,384},{8,392},{16,400},{24,408},{32,416},{40,424},{48,432},{56,4... | collective-permute-start | bytes 73736 | tf_op jit(solution)/shard_map/ppermute | solution.py:283
  58.7 22.5 %copy-start = (bf16[3,3,128,128]{3,2,1,0:T(8,128)(2,1)S(1)}, bf16[3,3,128,128]{3,2,1,0:T(8,128)(2,1)}, u32[]{:S(2)}) copy-start(bf16[3,3,128,128]{3,2,1,0:T(8,128)(2,1)} %param.11) | copy-start | bytes 884740
  58.7 22.5 %copy-start.1 = (bf16[3,3,128,128]{3,2,1,0:T(8,128)(2,1)S(1)}, bf16[3,3,128,128]{3,2,1,0:T(8,128)(2,1)}, u32[]{:S(2)}) copy-start(bf16[3,3,128,128]{3,2,1,0:T(8,128)(2,1)} %param.14) | copy-start | bytes 884740
  58.7 22.5 %copy-start.5 = (f32[2,128]{1,0:T(2,128)S(1)}, f32[2,128]{1,0:T(2,128)}, u32[]{:S(2)}) copy-start(f32[2,128]{1,0:T(2,128)} %film_ref.3) | copy-start | bytes 3076
  58.7 22.5 %copy-start.6 = (f32[128]{0:T(128)S(1)}, f32[128]{0:T(128)}, u32[]{:S(2)}) copy-start(f32[128]{0:T(128)} %param.12) | copy-start | bytes 1540
  58.7 10.3 %all-to-all-start.2 = ((bf16[8,48,256]{2,1,0:T(8,128)(2,1)}), bf16[8,48,256]{2,1,0:T(8,128)(2,1)S(1)}, u32[]{:S(2)}, u32[]{:S(2)}) async-start(bf16[8,48,256]{2,1,0:T(8,128)(2,1)} %shard_map.114), calls=%async_computation.2 | async-start | bytes 393216 | tf_op jit(solution)/shard_map/all_to_all | solution.py:294
  70.2 30.0 %all-to-all-start.3 = ((bf16[8,80,128]{2,1,0:T(8,128)(2,1)}), bf16[8,80,128]{2,1,0:T(8,128)(2,1)S(1)}, u32[]{:S(2)}, u32[]{:S(2)}) async-start(bf16[8,80,128]{2,1,0:T(8,128)(2,1)} %shard_map.115), calls=%async_computation.3 | async-start | bytes 327680 | tf_op jit(solution)/shard_map/all_to_all | solution.py:309
  81.2 19.0 %copy-start.4 = (bf16[1,48,128]{2,1,0:T(8,128)(2,1)S(1)}, bf16[1,48,128]{2,1,0:T(8,128)(2,1)}, u32[]{:S(2)}) copy-start(bf16[1,48,128]{2,1,0:T(8,128)(2,1)} %param.15) | copy-start | bytes 36868

commit v3 on v2

--- a/solution.py
+++ b/solution.py
@@ -15,7 +15,7 @@
 
 def lat_groups():
     place = lambda x, z, c: x * 16 + z * 2 + c
-    over_z = [[place(x, z, c) for z in range(8)] for x in range(4) for c in range(2)]
+    over_z = [[place(x, z, c) for z in (4, 3, 5, 2, 6, 1, 7, 0)] for x in range(4) for c in range(2)]
     over_xc = [[place(x, z, c) for x in range(4) for c in range(2)] for z in range(8)]
     return over_z, over_xc
 
@@ -42,8 +42,19 @@
     )
 
 
+def spread_body(flags_ref, given_ref, out_ref):
+    lons, total = out_ref.shape[:2]
+    half = given_ref.shape[0] - total
+    rows = total - half
+    first, last = given_ref[rows:total].astype(F32), given_ref[total:].astype(F32)
+    for j in range(lons):
+        out_ref[j, :rows] = given_ref[:rows]
+        out_ref[j, rows:] = jnp.where(lax.rem(flags_ref[3] + 1 + lons // 2, lons) == j, last, first).astype(BF16)
+
+
 def project_body(tokens_ref, weight_ref, q_ref, kv_ref):
-    wide = jnp.concatenate([tokens_ref[j] for j in range(tokens_ref.shape[0])], axis=1).astype(F32)
+    rows = q_ref.shape[0]
+    wide = jnp.concatenate([tokens_ref[(j + tokens_ref.shape[0] // 2) % tokens_ref.shape[0], :rows] for j in range(tokens_ref.shape[0])], axis=1).astype(F32)
     normed = (wide * lax.rsqrt(jnp.mean(wide * wide, axis=-1, keepdims=True) + 1e-06)).astype(BF16)
     q_width = q_ref.shape[1]
     flat = jnp.dot(normed, weight_ref[...], preferred_element_type=F32).astype(BF16)
@@ -53,11 +64,11 @@
         kv_ref[j] = kv
 
 
-def attend_body(place_ref, q0_ref, q1_ref, q2_ref, q3_ref, kv_ref, o_ref):
-    sources = (q0_ref, q1_ref, q2_ref, q3_ref)
-    cores, rows, width = q0_ref.shape
-    n = cores * len(sources)
-    q = jnp.concatenate([ref[t] for ref in sources for t in range(cores)], axis=0)
+def attend_body(flags_ref, own_ref, other_ref, kv_ref, o_ref):
+    rows, width = own_ref.shape[1:]
+    q = jnp.concatenate([own_ref[...], other_ref[...]], axis=0)
+    n = q.shape[0]
+    q = q.reshape(n * rows, width)
     kv = kv_ref[...].reshape(kv_ref.shape[0] * kv_ref.shape[1], 2 * width)
     scale = 1.0 / HEAD**0.5
     outs = []
@@ -78,14 +89,15 @@
             rest = rest - piece
             tail = jnp.where(lane == 3 * h + part, piece, tail)
     result = jnp.concatenate(outs + [tail], axis=1).astype(BF16)
-    x, core = place_ref[0], place_ref[1]
-    for s in range(len(sources)):
-        for t in range(cores):
-            at = lax.rem(x + s, len(sources)) * cores + (core if t == 0 else 1 - core)
-            o_ref[at] = result[(s * cores + t) * rows : (s * cores + t + 1) * rows]
-
-
-def merge_body(lon_ref, o_ref, wo_ref, first_ref, last_ref, out_ref):
+    x, core = flags_ref[4], flags_ref[5]
+    for t in range(2):
+        for s, chip in enumerate((x, x ^ 1, 3 - x, (3 - x) ^ 1)):
+            o_ref[2 * chip + (core ^ t)] = result[(4 * t + s) * rows : (4 * t + s + 1) * rows]
+
+
+def merge_body(flags_ref, o_ref, wo_hbm, first_ref, last_ref, out_ref, wo_ref, wo_sem):
+    copy = pltpu.make_async_copy(wo_hbm, wo_ref, wo_sem)
+    copy.start()
     n, rows, width = o_ref.shape[0], o_ref.shape[1], o_ref.shape[2] // 2
     heads = []
     for h in range(width // HEAD):
@@ -102,12 +114,14 @@
             num = num + weight * o_ref[p, :, h * HEAD : (h + 1) * HEAD].astype(F32)
         heads.append(num / total)
     attended = jnp.concatenate(heads, axis=1).astype(BF16)
+    copy.wait()
     partial = jnp.dot(attended, wo_ref[...], preferred_element_type=F32).astype(BF16)
     lons = out_ref.shape[0]
     first, last = first_ref[...].astype(F32), last_ref[...].astype(F32)
     for j in range(lons):
-        out_ref[j, :rows] = partial[:, j * width : (j + 1) * width]
-        out_ref[j, rows:] = jnp.where(lax.rem(lon_ref[0] + 1, lons) == j, last, first).astype(BF16)
+        at = (j + lons // 2) % lons
+        out_ref[at, :rows] = partial[:, j * width : (j + 1) * width]
+        out_ref[at, rows:] = jnp.where(lax.rem(flags_ref[3] + 1, lons) == j, last, first).astype(BF16)
 
 
 def three(row):
@@ -178,6 +192,7 @@
 def finish_body(
     flags_ref,
     parts_ref,
+    incoming_ref,
     tokens_ref,
     main_ref,
     strip_ref,
@@ -200,13 +215,16 @@
         shared = shared + parts_ref[j, :rows].astype(F32)
     tokens_out_ref[...] = (tokens_ref[...].astype(F32) + shared).astype(BF16)
 
-    left = parts_ref[lax.rem(lon + lons - 1, lons), rows:].astype(F32)
-    right = parts_ref[lax.rem(lon + 1, lons), rows:].astype(F32)
+    before, after = lax.rem(lon + lons - 1, lons), lax.rem(lon + 1, lons)
+    corners = [parts_ref[lax.rem(at + lons // 2, lons), rows:].astype(F32) for at in (after, before)]
+    sides = [incoming_ref[lax.rem(at + lons // 2, lons), rows:].astype(F32) for at in (after, before)]
     tall = strip_ref.shape[0]
 
     def ringed(i):
+        inside = 2 <= i < tall - 2
+        held, at, step = (sides, i - 2, height) if inside else (corners, i if i < 2 else i - height, 4)
         return jnp.concatenate(
-            [strip_ref[i].astype(F32)] + [side[c * tall + i : c * tall + i + 1] for side in (right, left) for c in range(2)]
+            [strip_ref[i].astype(F32)] + [side[c * step + at : c * step + at + 1] for side in held for c in range(2)]
         )
 
     windows(
@@ -256,15 +274,29 @@
     height, width, channels = field.shape
     rows = tokens.shape[0]
 
-    incoming = lax.all_to_all(jnp.broadcast_to(tokens[None], (lons,) + tokens.shape), "lon", 0, 0)
-
     even = lat % 2 == 0
+    step = lats // 4
+    flags = jnp.stack([lat == 0, lat == lats - 1, even, lon, lat // step, lat % 2]).astype(jnp.int32)
+
+    turned = [[(j + lons // 2) % lons for j in range(lons)]]
+    smem, vmem = pl.BlockSpec(memory_space=pltpu.SMEM), pl.BlockSpec(memory_space=pltpu.VMEM)
+    params = pltpu.CompilerParams(vmem_limit_bytes=VMEM_LIMIT)
+    column = lambda c: field[:, c]
+    spread = pl.pallas_call(
+        spread_body,
+        in_specs=[smem, vmem],
+        out_shape=jax.ShapeDtypeStruct((lons, rows + 2 * height, channels), BF16),
+        compiler_params=params,
+    )(
+        flags,
+        jnp.concatenate([tokens] + [column(c) for c in (0, 1, width - 2, width - 1)]),
+    )
+    incoming = lax.all_to_all(spread, "lon", 0, 0, axis_index_groups=turned)
+
     weights = jnp.concatenate([query_weight, key_weight, value_weight], axis=1)
-    upper, lower, weights = lax.optimization_barrier((field[:2], field[-2:], weights))
+    upper, lower, weights, flags = lax.optimization_barrier((field[:2], field[-2:], weights, flags))
     from_inner = lax.ppermute(jnp.where(even, lower, upper), ("lat", "lon"), inner)
     from_outer = lax.ppermute(jnp.where(even, upper, lower), ("lat", "lon"), outer)
-    above = jnp.where(even, from_outer, from_inner)
-    below = jnp.where(even, from_inner, from_outer)
 
     heads_width = query_weight.shape[1]
     n_z, n_xc = len(over_z[0]), len(over_xc[0])
@@ -276,39 +308,40 @@
         ),
     )(incoming, weights)
     pairs = lax.all_to_all(pairs, "lat", 0, 0, axis_index_groups=over_z)
-    other = lax.ppermute(queries, "lat", [(i, i ^ 1) for i in range(lats)])
-    chip = jnp.stack([queries, other])
-    step = lats // 4
-    gathered = [chip] + [
-        lax.ppermute(chip, "lat", [(i, (i - s * step) % lats) for i in range(lats)]) for s in range(1, 4)
-    ]
-
-    place = jnp.stack([lat // step, lat % 2]).astype(jnp.int32)
+    swap = lambda v, to: lax.ppermute(v, "lat", [(i, to(i // step) * step + i % step) for i in range(lats)])
+    near = swap(queries, lambda x: x ^ 1)
+    from_inner, from_outer, near = lax.optimization_barrier((from_inner, from_outer, near))
+    above = jnp.where(even, from_outer, from_inner)
+    below = jnp.where(even, from_inner, from_outer)
+    two = jnp.stack([queries, near])
+    own = jnp.concatenate([two, swap(two, lambda x: 3 - x)])
+    other = lax.ppermute(own, "lat", [(i, i ^ 1) for i in range(lats)])
+
+    side = 6
+    ends = lambda rows: jnp.concatenate([rows[:, :side], rows[:, -side:]], axis=1)
+    corners = jnp.concatenate([ends(above), ends(below)])
+    strip = jnp.concatenate([corners[:2], ends(field), corners[2:]])
+    first_columns = jnp.concatenate([corners[:, 0], corners[:, 1]])
+    last_columns = jnp.concatenate([corners[:, -2], corners[:, -1]])
+    first_columns, last_columns, own = lax.optimization_barrier((first_columns, last_columns, own))
+
     partial = pl.pallas_call(
         attend_body,
-        in_specs=[pl.BlockSpec(memory_space=pltpu.SMEM)] + [pl.BlockSpec(memory_space=pltpu.VMEM)] * 5,
+        in_specs=[pl.BlockSpec(memory_space=pltpu.SMEM)] + [pl.BlockSpec(memory_space=pltpu.VMEM)] * 3,
         out_shape=jax.ShapeDtypeStruct((n_xc, rows, 2 * heads_width), BF16),
         compiler_params=pltpu.CompilerParams(vmem_limit_bytes=VMEM_LIMIT),
-    )(place, *gathered, pairs)
+    )(flags, own, other, pairs)
 
     partial = lax.all_to_all(partial, "lat", 0, 0, axis_index_groups=over_xc)
-    side = 6
-    ends = lambda rows: jnp.concatenate([rows[:, :side], rows[:, -side:]], axis=1)
-    strip = jnp.concatenate([ends(above), ends(field), ends(below)])
-    tall = height + 4
-    first_columns = jnp.concatenate([strip[:, 0], strip[:, 1]])
-    last_columns = jnp.concatenate([strip[:, -2], strip[:, -1]])
-    smem, vmem = pl.BlockSpec(memory_space=pltpu.SMEM), pl.BlockSpec(memory_space=pltpu.VMEM)
-    params = pltpu.CompilerParams(vmem_limit_bytes=VMEM_LIMIT)
     projected = pl.pallas_call(
         merge_body,
-        in_specs=[smem] + [vmem] * 4,
-        out_shape=jax.ShapeDtypeStruct((lons, rows + 2 * tall, out_weight.shape[1] // lons), BF16),
+        in_specs=[smem, vmem, pl.BlockSpec(memory_space=pl.ANY), vmem, vmem],
+        out_shape=jax.ShapeDtypeStruct((lons, rows + first_columns.shape[0], out_weight.shape[1] // lons), BF16),
+        scratch_shapes=[pltpu.VMEM(out_weight.shape, BF16), pltpu.SemaphoreType.DMA],
         compiler_params=params,
-    )(lon.reshape(1).astype(jnp.int32), partial, out_weight, first_columns, last_columns)
-    projected = lax.all_to_all(projected, "lon", 0, 0)
-
-    flags = jnp.stack([lat == 0, lat == lats - 1, even, lon]).astype(jnp.int32)
+    )(flags, partial, out_weight, first_columns, last_columns)
+    projected = lax.all_to_all(projected, "lon", 0, 0, axis_index_groups=turned)
+
     kernels = (
         conv_first.reshape(3, 3 * channels, channels),
         bias_first.reshape(1, channels),
@@ -328,14 +361,14 @@
     )(flags, field, from_inner, from_outer, *kernels)
     bottleneck_out, fine_out = pl.pallas_call(
         finish_body,
-        in_specs=[smem] + [vmem] * 8,
+        in_specs=[smem] + [vmem] * 9,
         out_shape=(jax.ShapeDtypeStruct(tokens.shape, BF16), jax.ShapeDtypeStruct(field.shape, BF16)),
         scratch_shapes=[
             pltpu.VMEM((height + 8, 2 * side + 4, 3 * channels), BF16),
             pltpu.VMEM((height + 2, 2 * side + 4, 3 * channels), BF16),
         ],
         compiler_params=params,
-    )(flags, projected, tokens, main, strip, *kernels)
+    )(flags, projected, incoming, tokens, main, strip, *kernels)
     return (fine_out[None], bottleneck_out[None])
 
 

time: 103 us -> 90.9 us (0.88)
  the two profiles are of different devices: /device:TPU:192 before, /device:TPU:1 now
where the time goes in v3:
time: 90.9 us; the launch traced here: 90.1 us
  starting transfers between devices  61.2 us (67%)
  Pallas kernels  11.7 us (13%)
  blocking collectives  9.89 us (11%)
  waiting for transfers between devices  3.01 us (3%)
  local copies, waits for them, and re-layouts  2.08 us (2%)
  other arithmetic  1.24 us (1%)
  between operations  1.02 us (1%)
    all_to_all x1, starting transfers between devices, shards(): incoming = lax.all_to_all(spread, 'lon', 0, 0, axis_index_groups=turned)  18.6 us
    all_to_all x1, starting transfers between devices, shards(): projected = lax.all_to_all(projected, 'lon', 0, 0, axis_index_groups=turned)  13.9 us
    ppermute x2, starting transfers between devices, shards(): lax.ppermute(v, 'lat', [(i, to(i // step) * step + i % step) for i in ran...  12.8 us
    all_to_all x1, blocking collectives, shards(): partial = lax.all_to_all(partial, 'lat', 0, 0, axis_index_groups=over_xc)  9.89 us
    all_to_all x1, starting transfers between devices, shards(): pairs = lax.all_to_all(pairs, 'lat', 0, 0, axis_index_groups=over_z)  6.66 us
    pallas_call x1, Pallas kernels, shards(): pl.pallas_call(conv_body, in_specs=[smem] + [vmem] * 7, out_shape=jax.Sha...  4.22 us
    ppermute x1, starting transfers between devices, shards(): lax.ppermute(jnp.where(even, upper, lower), ('lat', 'lon'), outer)  3.77 us
    ppermute x1, starting transfers between devices, shards(): other = lax.ppermute(own, 'lat', [(i, i ^ 1) for i in range(lats)])  3.62 us
  transfers between devices with their start and end apart: 8, of which 2 were waited for; matrix products, arithmetic and copies ran while one was open for 1% of the time, Pallas kernels for 6%

profile of v3, /device:TPU:1, one launch (start us, length us, event | category | flops | bytes accessed | tf_op | source)
XLA Modules:
  0.0 90.1 jit_solution(12737485846320931566)
XLA Ops:
  0.6 0.0 copy-start.7
  0.6 0.0 copy-start.8
  0.7 1.0 %fusion.2 = (bf16[12,1,128]{2,1,0:T(2,128)(2,1)S(1)}, bf16[12,1,128]{2,1,0:T(2,128)(2,1)S(1)}, bf16[12,1,128]{2,1,0:T(2,128)(2,1)S(1)}, bf16[12,1,128]{2,1,0:T(2,128)(2,1)S(1)}) fusion(bf16[12,180,128]{2,1,0:T(8,128)(2,1)} %bitcast.39), kind=kLoop, calls=%fused_computation.27 | loop fusion | bytes 24576 | tf_op jit(solution)/shard_map/slice | solution.py:284
  1.7 0.9 %concatenate.32.given_ref = bf16[96,128]{1,0:T(8,128)(2,1)S(1)} concatenate(bf16[48,128]{1,0:T(8,128)(2,1)} %bitcast.46, bf16[12,128]{1,0:T(8,128)(2,1)S(1)} %get-tuple-element.53, bf16[12,128]{1,0:T(8,128)(2,1)S(1)} %get-tuple-element.52, bf16[12,128]{1,0:T(8,128)(2,1)S(1)} %get-tuple-element.51, bf16[12,128]{1,0:T(8,128)(2,1)S(1)} %get-tuple-element.50), dimensions={0} | concatenate | bytes 49152 | tf_op jit(solution)/shard_map/concatenate | solution.py:292
  2.6 0.1 stack.48.flags_ref
  2.7 1.2 %shard_map.113 = bf16[8,72,128]{2,1,0:T(8,128)(2,1)} custom-call(s32[6]{0:T(128)S(1)} %stack.48.flags_ref, bf16[96,128]{1,0:T(8,128)(2,1)S(1)} %concatenate.32.given_ref), custom_call_target="tpu_custom_call" | custom-call | tf_op jit(solution)/shard_map/pallas_call | solution.py:285
  3.9 18.6 %all-to-all-start = ((bf16[8,72,128]{2,1,0:T(8,128)(2,1)}), bf16[8,72,128]{2,1,0:T(8,128)(2,1)S(1)}, u32[]{:S(2)}, u32[]{:S(2)}) async-start(bf16[8,72,128]{2,1,0:T(8,128)(2,1)} %shard_map.113), calls=%async_computation | async-start | bytes 294912 | tf_op jit(solution)/shard_map/all_to_all | solution.py:294
  22.5 0.0 copy-done.7
  22.5 0.0 copy-done.8
  22.5 0.0 copy-start
  22.5 1.1 %pad_maximum_fusion.weight_ref = bf16[1024,384]{1,0:T(8,128)(2,1)S(1)} fusion(bf16[1024,128]{1,0:T(8,128)(2,1)S(1)} %copy-done.7, bf16[1024,128]{1,0:T(8,128)(2,1)S(1)} %copy-done.8, bf16[1024,128]{1,0:T(8,128)(2,1)} %param.16), kind=kLoop, calls=%fused_computation | loop fusion | flops 2359296 | bytes 1572864 | tf_op jit(solution)/shard_map/concatenate | solution.py:296
  23.6 0.0 copy-done
  23.7 3.8 %collective-permute-start.1 = (bf16[2,180,128]{2,1,0:T(8,128)(2,1)S(1)}, bf16[2,180,128]{2,1,0:T(8,128)(2,1)S(1)}, u32[]{:S(2)}, u32[]{:S(2)}) collective-permute-start(bf16[2,180,128]{2,1,0:T(8,128)(2,1)S(1)} %get-tuple-element.40), channel_id=1, source_target_pairs={{0,4},{1,5},{2,6},{3,7},{4,0},{5,1},{6,2},{7,3},{8,16},{9,17},{10,... | collective-permute-start | bytes 276488 | tf_op jit(solution)/shard_map/ppermute | solution.py:299
  27.4 1.9 %collective-permute-start = (bf16[2,180,128]{2,1,0:T(8,128)(2,1)S(1)}, bf16[2,180,128]{2,1,0:T(8,128)(2,1)S(1)}, u32[]{:S(2)}, u32[]{:S(2)}) collective-permute-start(bf16[2,180,128]{2,1,0:T(8,128)(2,1)S(1)} %get-tuple-element.41), channel_id=1, source_target_pairs={{0,8},{1,9},{2,10},{3,11},{4,12},{5,13},{6,14},{7,15},{8,0},{9,1},... | collective-permute-start | bytes 276488 | tf_op jit(solution)/shard_map/ppermute | solution.py:298
  29.4 0.0 all-to-all-done.tokens_ref.incoming_ref
  29.4 1.0 %shard_map.114 = (bf16[48,128]{1,0:T(8,128)(2,1)S(1)}, bf16[8,48,256]{2,1,0:T(8,128)(2,1)}) custom-call(bf16[8,72,128]{2,1,0:T(8,128)(2,1)S(1)} %all-to-all-done.tokens_ref.incoming_ref, bf16[1024,384]{1,0:T(8,128)(2,1)S(1)} %pad_maximum_fusion.weight_ref), custom_call_target="tpu_custom_call" | custom-call | tf_op jit(solution)/shard_map/pallas_call | solution.py:303
  30.4 8.9 %collective-permute-start.2 = (bf16[48,128]{1,0:T(8,128)(2,1)S(1)}, bf16[48,128]{1,0:T(8,128)(2,1)S(1)}, u32[]{:S(2)}, u32[]{:S(2)}) collective-permute-start(bf16[48,128]{1,0:T(8,128)(2,1)S(1)} %get-tuple-element.20), channel_id=1, source_target_pairs={{0,128},{8,136},{16,144},{24,152},{32,160},{40,168},{48,176},{56,1... | collective-permute-start | bytes 36872 | tf_op jit(solution)/shard_map/ppermute | solution.py:311
  39.3 6.7 %all-to-all-start.1 = ((bf16[8,48,256]{2,1,0:T(8,128)(2,1)}), bf16[8,48,256]{2,1,0:T(8,128)(2,1)S(1)}, u32[]{:S(2)}, u32[]{:S(2)}) async-start(bf16[8,48,256]{2,1,0:T(8,128)(2,1)} %get-tuple-element.25), calls=%async_computation.1 | async-start | bytes 393216 | tf_op jit(solution)/shard_map/all_to_all | solution.py:310
  46.0 0.0 copy-start.3
  46.0 0.0 collective-permute-done.1.outer_ref
  46.0 0.0 collective-permute-done.inner_ref
  46.0 0.0 collective-permute-done.2
  46.0 3.9 %collective-permute-start.3 = (bf16[2,48,128]{2,1,0:T(8,128)(2,1)S(1)}, bf16[2,48,128]{2,1,0:T(8,128)(2,1)S(1)}, u32[]{:S(2)}, u32[]{:S(2)}) collective-permute-start(bf16[2,48,128]{2,1,0:T(8,128)(2,1)S(1)} %pad_maximum_fusion.2), channel_id=1, source_target_pairs={{0,384},{8,392},{16,400},{24,408},{32,416},{40,424},{48,432},{56,4... | collective-permute-start | bytes 73736 | tf_op jit(solution)/shard_map/ppermute | solution.py:311
  50.0 2.2 %collective-permute-done.3 = bf16[2,48,128]{2,1,0:T(8,128)(2,1)S(1)} collective-permute-done((bf16[2,48,128]{2,1,0:T(8,128)(2,1)S(1)}, bf16[2,48,128]{2,1,0:T(8,128)(2,1)S(1)}, u32[]{:S(2)}, u32[]{:S(2)}) %collective-permute-start.3) | collective-permute-done | bytes 24608 | tf_op jit(solution)/shard_map/ppermute | solution.py:311
  52.2 3.6 %collective-permute-start.4 = (bf16[4,48,128]{2,1,0:T(8,128)(2,1)S(1)}, bf16[4,48,128]{2,1,0:T(8,128)(2,1)S(1)}, u32[]{:S(2)}, u32[]{:S(2)}) collective-permute-start(bf16[4,48,128]{2,1,0:T(8,128)(2,1)S(1)} %pad_maximum_fusion.1.own_ref), channel_id=1, source_target_pairs={{0,8},{8,0},{16,24},{24,16},{32,40},{40,32},{48,56},{56,48},{64,72... | collective-permute-start | bytes 147464 | tf_op jit(solution)/shard_map/ppermute | solution.py:318
  55.9 0.0 copy-start.1
  55.9 0.0 copy-start.2
  55.9 0.0 copy-start.5
  55.9 0.0 copy-start.6
  55.9 0.8 collective-permute-done.4.other_ref
  56.7 0.0 all-to-all-done.1.kv_ref
  56.7 1.6 %shard_map.115 = bf16[8,48,256]{2,1,0:T(8,128)(2,1)S(1)} custom-call(s32[6]{0:T(128)S(1)} %stack.48.flags_ref, bf16[4,48,128]{2,1,0:T(8,128)(2,1)S(1)} %pad_maximum_fusion.1.own_ref, bf16[4,48,128]{2,1,0:T(8,128)(2,1)S(1)} %collective-permute-done.4.other_ref, bf16[8,48,256]{2,1,0:T(8,128)(2,1)S(1)} %all-to-all-done.1.kv_ref), custom_call_target="tpu_custom_call" | custom-call | tf_op jit(solution)/shard_map/pallas_call | solution.py:328
  58.3 9.9 %all_to_all.20.o_ref = bf16[8,48,256]{2,1,0:T(8,128)(2,1)S(1)} all-to-all(bf16[8,48,256]{2,1,0:T(8,128)(2,1)S(1)} %shard_map.115), channel_id=1, replica_groups={{0,8,128,136,256,264,384,392},{16,24,144,152,272,280,400,408},{32,40,16..., dimensions={0} | all-to-all | bytes 393216 | tf_op jit(solution)/shard_map/all_to_all | solution.py:335
  68.2 0.0 copy-done.3
  68.2 1.7 %shard_map.116 = bf16[8,56,128]{2,1,0:T(8,128)(2,1)} custom-call(s32[6]{0:T(128)S(1)} %stack.48.flags_ref, bf16[8,48,256]{2,1,0:T(8,128)(2,1)S(1)} %all_to_all.20.o_ref, bf16[128,1024]{1,0:T(8,128)(2,1)S(1)} %copy-done.3, bf16[8,128]{1,0:T(8,128)(2,1)S(1)} %pad_maximum_fusion.5.first_ref, bf16[8,128]{1,0:T(8,128)(2,1)S(1)} %pad_maximum_fusion.6.last_ref), custom_call_target="tpu_custom_call" | custom-call | tf_op jit(solution)/shard_map/pallas_call | solution.py:336
  69.9 13.9 %all-to-all-start.3 = ((bf16[8,56,128]{2,1,0:T(8,128)(2,1)}), bf16[8,56,128]{2,1,0:T(8,128)(2,1)S(1)}, u32[]{:S(2)}, u32[]{:S(2)}) async-start(bf16[8,56,128]{2,1,0:T(8,128)(2,1)} %shard_map.116), calls=%async_computation.3 | async-start | bytes 229376 | tf_op jit(solution)/shard_map/all_to_all | solution.py:343
  83.8 0.0 copy-done.1
  83.8 0.0 copy-done.2
  83.8 0.0 copy-done.5
  83.8 0.0 copy-done.6
  83.8 0.0 copy-start.4
  83.8 4.2 %shard_map.117.main_ref = bf16[12,180,128]{2,1,0:T(8,128)(2,1)S(1)} custom-call(s32[6]{0:T(128)S(1)} %stack.48.flags_ref, bf16[12,180,128]{2,1,0:T(8,128)(2,1)S(1)} %bitcast.41, bf16[2,180,128]{2,1,0:T(8,128)(2,1)S(1)} %collective-permute-done.inner_ref, bf16[2,180,128]{2,1,0:T(8,128)(2,1)S(1)} %collective-permute-done.1.outer_ref, ...), custom_call_target="tpu_custom_call" | custom-call | tf_op jit(solution)/shard_map/pallas_call | solution.py:352
  88.1 0.0 all-to-all-done.3.parts_ref
  88.1 0.0 copy-done.4
  88.1 2.0 %shard_map.118 = (bf16[48,128]{1,0:T(8,128)(2,1)}, bf16[12,180,128]{2,1,0:T(8,128)(2,1)}) custom-call(s32[6]{0:T(128)S(1)} %stack.48.flags_ref, bf16[8,56,128]{2,1,0:T(8,128)(2,1)S(1)} %all-to-all-done.3.parts_ref, bf16[8,72,128]{2,1,0:T(8,128)(2,1)S(1)} %all-to-all-done.tokens_ref.incoming_ref, bf16[48,128]{1,0:T(8,128)(2,1)S(1)} %bitcast.47, ...), custom_call_target="tpu_custom_call" | custom-call | tf_op jit(solution)/shard_map/pallas_call | solution.py:362
  (18 shorter events, 0.2 us)
Async XLA Ops:
  0.6 21.8 %copy-start.7 = (bf16[1024,128]{1,0:T(8,128)(2,1)S(1)}, bf16[1024,128]{1,0:T(8,128)(2,1)}, u32[]{:S(2)}) copy-start(bf16[1024,128]{1,0:T(8,128)(2,1)} %param.18) | copy-start | bytes 786436
  0.6 21.8 %copy-start.8 = (bf16[1024,128]{1,0:T(8,128)(2,1)S(1)}, bf16[1024,128]{1,0:T(8,128)(2,1)}, u32[]{:S(2)}) copy-start(bf16[1024,128]{1,0:T(8,128)(2,1)} %param.17) | copy-start | bytes 786436
  3.9 25.5 %all-to-all-start = ((bf16[8,72,128]{2,1,0:T(8,128)(2,1)}), bf16[8,72,128]{2,1,0:T(8,128)(2,1)S(1)}, u32[]{:S(2)}, u32[]{:S(2)}) async-start(bf16[8,72,128]{2,1,0:T(8,128)(2,1)} %shard_map.113), calls=%async_computation | async-start | bytes 294912 | tf_op jit(solution)/shard_map/all_to_all | solution.py:294
  22.5 1.1 %copy-start = (bf16[1,12,180,128]{3,2,1,0:T(8,128)(2,1)S(1)}, bf16[1,12,180,128]{3,2,1,0:T(8,128)(2,1)}, u32[]{:S(2)}) copy-start(bf16[1,12,180,128]{3,2,1,0:T(8,128)(2,1)} %param.10) | copy-start | bytes 1658884
  23.7 22.3 %collective-permute-start.1 = (bf16[2,180,128]{2,1,0:T(8,128)(2,1)S(1)}, bf16[2,180,128]{2,1,0:T(8,128)(2,1)S(1)}, u32[]{:S(2)}, u32[]{:S(2)}) collective-permute-start(bf16[2,180,128]{2,1,0:T(8,128)(2,1)S(1)} %get-tuple-element.40), channel_id=1, source_target_pairs={{0,4},{1,5},{2,6},{3,7},{4,0},{5,1},{6,2},{7,3},{8,16},{9,17},{10,... | collective-permute-start | bytes 276488 | tf_op jit(solution)/shard_map/ppermute | solution.py:299
  27.4 18.5 %collective-permute-start = (bf16[2,180,128]{2,1,0:T(8,128)(2,1)S(1)}, bf16[2,180,128]{2,1,0:T(8,128)(2,1)S(1)}, u32[]{:S(2)}, u32[]{:S(2)}) collective-permute-start(bf16[2,180,128]{2,1,0:T(8,128)(2,1)S(1)} %get-tuple-element.41), channel_id=1, source_target_pairs={{0,8},{1,9},{2,10},{3,11},{4,12},{5,13},{6,14},{7,15},{8,0},{9,1},... | collective-permute-start | bytes 276488 | tf_op jit(solution)/shard_map/ppermute | solution.py:298
  30.4 15.6 %collective-permute-start.2 = (bf16[48,128]{1,0:T(8,128)(2,1)S(1)}, bf16[48,128]{1,0:T(8,128)(2,1)S(1)}, u32[]{:S(2)}, u32[]{:S(2)}) collective-permute-start(bf16[48,128]{1,0:T(8,128)(2,1)S(1)} %get-tuple-element.20), channel_id=1, source_target_pairs={{0,128},{8,136},{16,144},{24,152},{32,160},{40,168},{48,176},{56,1... | collective-permute-start | bytes 36872 | tf_op jit(solution)/shard_map/ppermute | solution.py:311
  39.3 17.4 %all-to-all-start.1 = ((bf16[8,48,256]{2,1,0:T(8,128)(2,1)}), bf16[8,48,256]{2,1,0:T(8,128)(2,1)S(1)}, u32[]{:S(2)}, u32[]{:S(2)}) async-start(bf16[8,48,256]{2,1,0:T(8,128)(2,1)} %get-tuple-element.25), calls=%async_computation.1 | async-start | bytes 393216 | tf_op jit(solution)/shard_map/all_to_all | solution.py:310
  46.0 22.2 %copy-start.3 = (bf16[128,1024]{1,0:T(8,128)(2,1)S(1)}, bf16[128,1024]{1,0:T(8,128)(2,1)}, u32[]{:S(2)}) copy-start(bf16[128,1024]{1,0:T(8,128)(2,1)} %wo_hbm.1) | copy-start | bytes 786436
  46.0 6.2 %collective-permute-start.3 = (bf16[2,48,128]{2,1,0:T(8,128)(2,1)S(1)}, bf16[2,48,128]{2,1,0:T(8,128)(2,1)S(1)}, u32[]{:S(2)}, u32[]{:S(2)}) collective-permute-start(bf16[2,48,128]{2,1,0:T(8,128)(2,1)S(1)} %pad_maximum_fusion.2), channel_id=1, source_target_pairs={{0,384},{8,392},{16,400},{24,408},{32,416},{40,424},{48,432},{56,4... | collective-permute-start | bytes 73736 | tf_op jit(solution)/shard_map/ppermute | solution.py:311
  52.2 4.5 %collective-permute-start.4 = (bf16[4,48,128]{2,1,0:T(8,128)(2,1)S(1)}, bf16[4,48,128]{2,1,0:T(8,128)(2,1)S(1)}, u32[]{:S(2)}, u32[]{:S(2)}) collective-permute-start(bf16[4,48,128]{2,1,0:T(8,128)(2,1)S(1)} %pad_maximum_fusion.1.own_ref), channel_id=1, source_target_pairs={{0,8},{8,0},{16,24},{24,16},{32,40},{40,32},{48,56},{56,48},{64,72... | collective-permute-start | bytes 147464 | tf_op jit(solution)/shard_map/ppermute | solution.py:318
  55.9 27.9 %copy-start.1 = (bf16[3,3,128,128]{3,2,1,0:T(8,128)(2,1)S(1)}, bf16[3,3,128,128]{3,2,1,0:T(8,128)(2,1)}, u32[]{:S(2)}) copy-start(bf16[3,3,128,128]{3,2,1,0:T(8,128)(2,1)} %param.11) | copy-start | bytes 884740
  55.9 27.9 %copy-start.2 = (bf16[3,3,128,128]{3,2,1,0:T(8,128)(2,1)S(1)}, bf16[3,3,128,128]{3,2,1,0:T(8,128)(2,1)}, u32[]{:S(2)}) copy-start(bf16[3,3,128,128]{3,2,1,0:T(8,128)(2,1)} %param.14) | copy-start | bytes 884740
  55.9 27.9 %copy-start.5 = (f32[2,128]{1,0:T(2,128)S(1)}, f32[2,128]{1,0:T(2,128)}, u32[]{:S(2)}) copy-start(f32[2,128]{1,0:T(2,128)} %film_ref.3) | copy-start | bytes 3076
  55.9 27.9 %copy-start.6 = (f32[128]{0:T(128)S(1)}, f32[128]{0:T(128)}, u32[]{:S(2)}) copy-start(f32[128]{0:T(128)} %param.12) | copy-start | bytes 1540
  69.9 18.2 %all-to-all-start.3 = ((bf16[8,56,128]{2,1,0:T(8,128)(2,1)}), bf16[8,56,128]{2,1,0:T(8,128)(2,1)S(1)}, u32[]{:S(2)}, u32[]{:S(2)}) async-start(bf16[8,56,128]{2,1,0:T(8,128)(2,1)} %shard_map.116), calls=%async_computation.3 | async-start | bytes 229376 | tf_op jit(solution)/shard_map/all_to_all | solution.py:343
  83.8 4.3 %copy-start.4 = (bf16[1,48,128]{2,1,0:T(8,128)(2,1)S(1)}, bf16[1,48,128]{2,1,0:T(8,128)(2,1)}, u32[]{:S(2)}) copy-start(bf16[1,48,128]{2,1,0:T(8,128)(2,1)} %param.15) | copy-start | bytes 36868

commit v4 on v3

--- a/solution.py
+++ b/solution.py
@@ -33,6 +33,14 @@
     return inner, outer
 
 
+def place_here():
+    return lax.axis_index("lat"), lax.axis_index("lon")
+
+
+def spot(lon):
+    return 7 - lon
+
+
 def kernel_call(body, out_shape, **extra):
     return pl.pallas_call(
         body,
@@ -42,19 +50,23 @@
     )
 
 
-def spread_body(flags_ref, given_ref, out_ref):
+def spread_body(tokens_hbm, given_ref, out_ref, tokens_ref, sem):
+    copy = pltpu.make_async_copy(tokens_hbm, tokens_ref, sem)
+    copy.start()
+    lon = place_here()[1]
     lons, total = out_ref.shape[:2]
-    half = given_ref.shape[0] - total
-    rows = total - half
-    first, last = given_ref[rows:total].astype(F32), given_ref[total:].astype(F32)
+    rows = tokens_ref.shape[0]
+    first, last = given_ref[: total - rows].astype(F32), given_ref[total - rows :].astype(F32)
     for j in range(lons):
-        out_ref[j, :rows] = given_ref[:rows]
-        out_ref[j, rows:] = jnp.where(lax.rem(flags_ref[3] + 1 + lons // 2, lons) == j, last, first).astype(BF16)
+        out_ref[j, rows:] = jnp.where(spot(lax.rem(lon + 1, lons)) == j, last, first).astype(BF16)
+    copy.wait()
+    for j in range(lons):
+        out_ref[j, :rows] = tokens_ref[...]
 
 
 def project_body(tokens_ref, weight_ref, q_ref, kv_ref):
     rows = q_ref.shape[0]
-    wide = jnp.concatenate([tokens_ref[(j + tokens_ref.shape[0] // 2) % tokens_ref.shape[0], :rows] for j in range(tokens_ref.shape[0])], axis=1).astype(F32)
+    wide = jnp.concatenate([tokens_ref[spot(j), :rows] for j in range(tokens_ref.shape[0])], axis=1).astype(F32)
     normed = (wide * lax.rsqrt(jnp.mean(wide * wide, axis=-1, keepdims=True) + 1e-06)).astype(BF16)
     q_width = q_ref.shape[1]
     flat = jnp.dot(normed, weight_ref[...], preferred_element_type=F32).astype(BF16)
@@ -64,7 +76,7 @@
         kv_ref[j] = kv
 
 
-def attend_body(flags_ref, own_ref, other_ref, kv_ref, o_ref):
+def attend_body(own_ref, other_ref, kv_ref, o_ref):
     rows, width = own_ref.shape[1:]
     q = jnp.concatenate([own_ref[...], other_ref[...]], axis=0)
     n = q.shape[0]
@@ -89,15 +101,15 @@
             rest = rest - piece
             tail = jnp.where(lane == 3 * h + part, piece, tail)
     result = jnp.concatenate(outs + [tail], axis=1).astype(BF16)
-    x, core = flags_ref[4], flags_ref[5]
+    lat = place_here()[0]
+    x, core = lat // 16, lax.rem(lat, 2)
     for t in range(2):
         for s, chip in enumerate((x, x ^ 1, 3 - x, (3 - x) ^ 1)):
             o_ref[2 * chip + (core ^ t)] = result[(4 * t + s) * rows : (4 * t + s + 1) * rows]
 
 
-def merge_body(flags_ref, o_ref, wo_hbm, first_ref, last_ref, out_ref, wo_ref, wo_sem):
-    copy = pltpu.make_async_copy(wo_hbm, wo_ref, wo_sem)
-    copy.start()
+def merge_body(o_ref, wo_ref, first_ref, last_ref, out_ref):
+    lon = place_here()[1]
     n, rows, width = o_ref.shape[0], o_ref.shape[1], o_ref.shape[2] // 2
     heads = []
     for h in range(width // HEAD):
@@ -114,14 +126,13 @@
             num = num + weight * o_ref[p, :, h * HEAD : (h + 1) * HEAD].astype(F32)
         heads.append(num / total)
     attended = jnp.concatenate(heads, axis=1).astype(BF16)
-    copy.wait()
     partial = jnp.dot(attended, wo_ref[...], preferred_element_type=F32).astype(BF16)
     lons = out_ref.shape[0]
     first, last = first_ref[...].astype(F32), last_ref[...].astype(F32)
     for j in range(lons):
-        at = (j + lons // 2) % lons
+        at = spot(j)
         out_ref[at, :rows] = partial[:, j * width : (j + 1) * width]
-        out_ref[at, rows:] = jnp.where(lax.rem(flags_ref[3] + 1, lons) == j, last, first).astype(BF16)
+        out_ref[at, rows:] = jnp.where(lax.rem(lon + 1, lons) == j, last, first).astype(BF16)
 
 
 def three(row):
@@ -158,11 +169,12 @@
 
 
 def conv_body(
-    flags_ref, field_ref, inner_ref, outer_ref, first_ref, bias_ref, film_ref, second_ref, out_ref, wide_ref, hidden_ref
+    field_ref, inner_ref, outer_ref, first_ref, bias_ref, film_ref, second_ref, out_ref, wide_ref, hidden_ref
 ):
     height, width, channels = field_ref.shape
     ring = wide_ref.shape[1]
-    north, south, even = (flags_ref[i] == 1 for i in range(3))
+    lat = place_here()[0]
+    north, south, even = lat == 0, lat == lax.axis_size("lat") - 1, lax.rem(lat, 2) == 0
     gap = jnp.zeros((ring - width, channels), F32)
 
     def ringed(row):
@@ -190,7 +202,6 @@
 
 
 def finish_body(
-    flags_ref,
     parts_ref,
     incoming_ref,
     tokens_ref,
@@ -209,15 +220,16 @@
     rows = tokens_ref.shape[0]
     height, width, _ = main_ref.shape
     ring = wide_ref.shape[1]
-    north, south, lon = flags_ref[0] == 1, flags_ref[1] == 1, flags_ref[3]
+    lat, lon = place_here()
+    north, south = lat == 0, lat == lax.axis_size("lat") - 1
     shared = parts_ref[0, :rows].astype(F32)
     for j in range(1, lons):
         shared = shared + parts_ref[j, :rows].astype(F32)
     tokens_out_ref[...] = (tokens_ref[...].astype(F32) + shared).astype(BF16)
 
     before, after = lax.rem(lon + lons - 1, lons), lax.rem(lon + 1, lons)
-    corners = [parts_ref[lax.rem(at + lons // 2, lons), rows:].astype(F32) for at in (after, before)]
-    sides = [incoming_ref[lax.rem(at + lons // 2, lons), rows:].astype(F32) for at in (after, before)]
+    corners = [parts_ref[spot(at), rows:].astype(F32) for at in (after, before)]
+    sides = [incoming_ref[spot(at), rows:].astype(F32) for at in (after, before)]
     tall = strip_ref.shape[0]
 
     def ringed(i):
@@ -276,25 +288,25 @@
 
     even = lat % 2 == 0
     step = lats // 4
-    flags = jnp.stack([lat == 0, lat == lats - 1, even, lon, lat // step, lat % 2]).astype(jnp.int32)
-
-    turned = [[(j + lons // 2) % lons for j in range(lons)]]
-    smem, vmem = pl.BlockSpec(memory_space=pltpu.SMEM), pl.BlockSpec(memory_space=pltpu.VMEM)
+
+    turned = [[7, 6, 5, 4, 3, 2, 1, 0]]
+    vmem = pl.BlockSpec(memory_space=pltpu.VMEM)
     params = pltpu.CompilerParams(vmem_limit_bytes=VMEM_LIMIT)
     column = lambda c: field[:, c]
     spread = pl.pallas_call(
         spread_body,
-        in_specs=[smem, vmem],
+        in_specs=[pl.BlockSpec(memory_space=pl.ANY), vmem],
         out_shape=jax.ShapeDtypeStruct((lons, rows + 2 * height, channels), BF16),
+        scratch_shapes=[pltpu.VMEM(tokens.shape, BF16), pltpu.SemaphoreType.DMA],
         compiler_params=params,
     )(
-        flags,
-        jnp.concatenate([tokens] + [column(c) for c in (0, 1, width - 2, width - 1)]),
+        tokens,
+        jnp.concatenate([column(c) for c in (0, 1, width - 2, width - 1)]),
     )
     incoming = lax.all_to_all(spread, "lon", 0, 0, axis_index_groups=turned)
 
     weights = jnp.concatenate([query_weight, key_weight, value_weight], axis=1)
-    upper, lower, weights, flags = lax.optimization_barrier((field[:2], field[-2:], weights, flags))
+    upper, lower, weights = lax.optimization_barrier((field[:2], field[-2:], weights))
     from_inner = lax.ppermute(jnp.where(even, lower, upper), ("lat", "lon"), inner)
     from_outer = lax.ppermute(jnp.where(even, upper, lower), ("lat", "lon"), outer)
 
@@ -327,19 +339,18 @@
 
     partial = pl.pallas_call(
         attend_body,
-        in_specs=[pl.BlockSpec(memory_space=pltpu.SMEM)] + [pl.BlockSpec(memory_space=pltpu.VMEM)] * 3,
+        in_specs=[pl.BlockSpec(memory_space=pltpu.VMEM)] * 3,
         out_shape=jax.ShapeDtypeStruct((n_xc, rows, 2 * heads_width), BF16),
         compiler_params=pltpu.CompilerParams(vmem_limit_bytes=VMEM_LIMIT),
-    )(flags, own, other, pairs)
+    )(own, other, pairs)
 
     partial = lax.all_to_all(partial, "lat", 0, 0, axis_index_groups=over_xc)
     projected = pl.pallas_call(
         merge_body,
-        in_specs=[smem, vmem, pl.BlockSpec(memory_space=pl.ANY), vmem, vmem],
+        in_specs=[vmem] * 4,
         out_shape=jax.ShapeDtypeStruct((lons, rows + first_columns.shape[0], out_weight.shape[1] // lons), BF16),
-        scratch_shapes=[pltpu.VMEM(out_weight.shape, BF16), pltpu.SemaphoreType.DMA],
         compiler_params=params,
-    )(flags, partial, out_weight, first_columns, last_columns)
+    )(partial, out_weight, first_columns, last_columns)
     projected = lax.all_to_all(projected, "lon", 0, 0, axis_index_groups=turned)
 
     kernels = (
@@ -351,24 +362,24 @@
     ring = -(-width // 16) * 16
     main = pl.pallas_call(
         conv_body,
-        in_specs=[smem] + [vmem] * 7,
+        in_specs=[vmem] * 7,
         out_shape=jax.ShapeDtypeStruct(field.shape, BF16),
         scratch_shapes=[
             pltpu.VMEM((height + 8, ring, 3 * channels), BF16),
             pltpu.VMEM((height + 2, ring, 3 * channels), BF16),
         ],
         compiler_params=params,
-    )(flags, field, from_inner, from_outer, *kernels)
+    )(field, from_inner, from_outer, *kernels)
     bottleneck_out, fine_out = pl.pallas_call(
         finish_body,
-        in_specs=[smem] + [vmem] * 9,
+        in_specs=[vmem] * 9,
         out_shape=(jax.ShapeDtypeStruct(tokens.shape, BF16), jax.ShapeDtypeStruct(field.shape, BF16)),
         scratch_shapes=[
             pltpu.VMEM((height + 8, 2 * side + 4, 3 * channels), BF16),
             pltpu.VMEM((height + 2, 2 * side + 4, 3 * channels), BF16),
         ],
         compiler_params=params,
-    )(flags, projected, incoming, tokens, main, strip, *kernels)
+    )(projected, incoming, tokens, main, strip, *kernels)
     return (fine_out[None], bottleneck_out[None])
 
 

time: 90.9 us -> 88.4 us (0.972)
  Pallas kernels: 11.7 us -> 8.96 us
    pallas_call x5, Pallas kernels: 10.7 us -> 7.97 us  [the longest x1 3.67 us: shards(): pl.pallas_call(conv_body, in_specs=[vmem] * 7, out_shape=jax.ShapeDtypeSt...]
    all_to_all x1, starting transfers between devices: 18.6 us -> 20.1 us  [shards(): incoming = lax.all_to_all(spread, 'lon', 0, 0, axis_index_groups=turned)]
    concatenate x1 -> x0, local copies, waits for them, and re-layouts: 0.92 us -> none  [shards(): jnp.concatenate([tokens] + [column(c) for c in (0, 1, width - 2, width -...]
  transfers between devices with their start and end apart: 8 -> 8, of which waited for: 2 -> 2; matrix products, arithmetic and copies ran while one was open for 1% -> 2% of each run, Pallas kernels for 6% -> 5%
where the time goes in v4:
time: 88.4 us; the launch traced here: 87.7 us
  starting transfers between devices  61.7 us (70%)
  blocking collectives  9.89 us (11%)
  Pallas kernels  8.96 us (10%)
  waiting for transfers between devices  3.01 us (3%)
  local copies, waits for them, and re-layouts  1.77 us (2%)
  other arithmetic  1.41 us (2%)
  between operations  0.95 us (1%)
    all_to_all x1, starting transfers between devices, shards(): incoming = lax.all_to_all(spread, 'lon', 0, 0, axis_index_groups=turned)  20.1 us
    all_to_all x1, starting transfers between devices, shards(): projected = lax.all_to_all(projected, 'lon', 0, 0, axis_index_groups=turned)  13.9 us
    ppermute x2, starting transfers between devices, shards(): lax.ppermute(v, 'lat', [(i, to(i // step) * step + i % step) for i in ran...  12 us
    all_to_all x1, blocking collectives, shards(): partial = lax.all_to_all(partial, 'lat', 0, 0, axis_index_groups=over_xc)  9.89 us
    all_to_all x1, starting transfers between devices, shards(): pairs = lax.all_to_all(pairs, 'lat', 0, 0, axis_index_groups=over_z)  6.66 us
    pallas_call x1, Pallas kernels, shards(): pl.pallas_call(conv_body, in_specs=[vmem] * 7, out_shape=jax.ShapeDtypeSt...  3.67 us
    ppermute x1, starting transfers between devices, shards(): other = lax.ppermute(own, 'lat', [(i, i ^ 1) for i in range(lats)])  3.62 us
    ppermute x1, starting transfers between devices, shards(): lax.ppermute(jnp.where(even, upper, lower), ('lat', 'lon'), outer)  3.49 us
  transfers between devices with their start and end apart: 8, of which 2 were waited for; matrix products, arithmetic and copies ran while one was open for 2% of the time, Pallas kernels for 5%

profile of v4, /device:TPU:1, one launch (start us, length us, event | category | flops | bytes accessed | tf_op | source)
XLA Modules:
  0.0 87.7 jit_solution(10648374323742950269)
XLA Ops:
  0.6 1.0 %fusion.2 = (bf16[12,1,128]{2,1,0:T(2,128)(2,1)S(1)}, bf16[12,1,128]{2,1,0:T(2,128)(2,1)S(1)}, bf16[12,1,128]{2,1,0:T(2,128)(2,1)S(1)}, bf16[12,1,128]{2,1,0:T(2,128)(2,1)S(1)}) fusion(bf16[12,180,128]{2,1,0:T(8,128)(2,1)} %bitcast.33), kind=kLoop, calls=%fused_computation.28 | loop fusion | bytes 24576 | tf_op jit(solution)/shard_map/slice | solution.py:295
  1.6 0.0 copy-start.4
  1.6 0.7 copy-done.4
  2.3 0.7 shard_map.113
  3.0 20.1 %all-to-all-start = ((bf16[8,72,128]{2,1,0:T(8,128)(2,1)}), bf16[8,72,128]{2,1,0:T(8,128)(2,1)S(1)}, u32[]{:S(2)}, u32[]{:S(2)}) async-start(bf16[8,72,128]{2,1,0:T(8,128)(2,1)} %shard_map.113), calls=%async_computation | async-start | bytes 294912 | tf_op jit(solution)/shard_map/all_to_all | solution.py:306
  23.2 0.0 copy-start
  23.2 1.3 %pad_maximum_fusion.weight_ref = bf16[1024,384]{1,0:T(8,128)(2,1)S(1)} fusion(bf16[1024,128]{1,0:T(8,128)(2,1)} %param.18, bf16[1024,128]{1,0:T(8,128)(2,1)} %param.17, bf16[1024,128]{1,0:T(8,128)(2,1)} %param.16), kind=kLoop, calls=%fused_computation | loop fusion | flops 2359296 | bytes 1572864 | tf_op jit(solution)/shard_map/concatenate | solution.py:308
  24.5 0.0 copy-done
  24.5 3.5 %collective-permute-start.1 = (bf16[2,180,128]{2,1,0:T(8,128)(2,1)S(1)}, bf16[2,180,128]{2,1,0:T(8,128)(2,1)S(1)}, u32[]{:S(2)}, u32[]{:S(2)}) collective-permute-start(bf16[2,180,128]{2,1,0:T(8,128)(2,1)S(1)} %get-tuple-element.38), channel_id=1, source_target_pairs={{0,4},{1,5},{2,6},{3,7},{4,0},{5,1},{6,2},{7,3},{8,16},{9,17},{10,... | collective-permute-start | bytes 276488 | tf_op jit(solution)/shard_map/ppermute | solution.py:311
  28.0 1.9 %collective-permute-start = (bf16[2,180,128]{2,1,0:T(8,128)(2,1)S(1)}, bf16[2,180,128]{2,1,0:T(8,128)(2,1)S(1)}, u32[]{:S(2)}, u32[]{:S(2)}) collective-permute-start(bf16[2,180,128]{2,1,0:T(8,128)(2,1)S(1)} %get-tuple-element.39), channel_id=1, source_target_pairs={{0,8},{1,9},{2,10},{3,11},{4,12},{5,13},{6,14},{7,15},{8,0},{9,1},... | collective-permute-start | bytes 276488 | tf_op jit(solution)/shard_map/ppermute | solution.py:310
  30.0 0.0 all-to-all-done.tokens_ref.incoming_ref
  30.0 1.0 %shard_map.114 = (bf16[48,128]{1,0:T(8,128)(2,1)S(1)}, bf16[8,48,256]{2,1,0:T(8,128)(2,1)}) custom-call(bf16[8,72,128]{2,1,0:T(8,128)(2,1)S(1)} %all-to-all-done.tokens_ref.incoming_ref, bf16[1024,384]{1,0:T(8,128)(2,1)S(1)} %pad_maximum_fusion.weight_ref), custom_call_target="tpu_custom_call" | custom-call | tf_op jit(solution)/shard_map/pallas_call | solution.py:315
  31.0 8.1 %collective-permute-start.2 = (bf16[48,128]{1,0:T(8,128)(2,1)S(1)}, bf16[48,128]{1,0:T(8,128)(2,1)S(1)}, u32[]{:S(2)}, u32[]{:S(2)}) collective-permute-start(bf16[48,128]{1,0:T(8,128)(2,1)S(1)} %get-tuple-element.18), channel_id=1, source_target_pairs={{0,128},{8,136},{16,144},{24,152},{32,160},{40,168},{48,176},{56,1... | collective-permute-start | bytes 36872 | tf_op jit(solution)/shard_map/ppermute | solution.py:323
  39.1 6.7 %all-to-all-start.1 = ((bf16[8,48,256]{2,1,0:T(8,128)(2,1)}), bf16[8,48,256]{2,1,0:T(8,128)(2,1)S(1)}, u32[]{:S(2)}, u32[]{:S(2)}) async-start(bf16[8,48,256]{2,1,0:T(8,128)(2,1)} %get-tuple-element.23), calls=%async_computation.1 | async-start | bytes 393216 | tf_op jit(solution)/shard_map/all_to_all | solution.py:322
  45.7 0.0 copy-start.3
  45.7 0.0 collective-permute-done.1.outer_ref
  45.8 0.0 collective-permute-done.inner_ref
  45.8 0.0 collective-permute-done.2
  45.8 3.9 %collective-permute-start.3 = (bf16[2,48,128]{2,1,0:T(8,128)(2,1)S(1)}, bf16[2,48,128]{2,1,0:T(8,128)(2,1)S(1)}, u32[]{:S(2)}, u32[]{:S(2)}) collective-permute-start(bf16[2,48,128]{2,1,0:T(8,128)(2,1)S(1)} %pad_maximum_fusion.2), channel_id=1, source_target_pairs={{0,384},{8,392},{16,400},{24,408},{32,416},{40,424},{48,432},{56,4... | collective-permute-start | bytes 73736 | tf_op jit(solution)/shard_map/ppermute | solution.py:323
  49.8 2.2 %collective-permute-done.3 = bf16[2,48,128]{2,1,0:T(8,128)(2,1)S(1)} collective-permute-done((bf16[2,48,128]{2,1,0:T(8,128)(2,1)S(1)}, bf16[2,48,128]{2,1,0:T(8,128)(2,1)S(1)}, u32[]{:S(2)}, u32[]{:S(2)}) %collective-permute-start.3) | collective-permute-done | bytes 24608 | tf_op jit(solution)/shard_map/ppermute | solution.py:323
  52.0 3.6 %collective-permute-start.4 = (bf16[4,48,128]{2,1,0:T(8,128)(2,1)S(1)}, bf16[4,48,128]{2,1,0:T(8,128)(2,1)S(1)}, u32[]{:S(2)}, u32[]{:S(2)}) collective-permute-start(bf16[4,48,128]{2,1,0:T(8,128)(2,1)S(1)} %pad_maximum_fusion.1.own_ref), channel_id=1, source_target_pairs={{0,8},{8,0},{16,24},{24,16},{32,40},{40,32},{48,56},{56,48},{64,72... | collective-permute-start | bytes 147464 | tf_op jit(solution)/shard_map/ppermute | solution.py:330
  55.6 0.0 copy-start.1
  55.7 0.0 copy-start.2
  55.7 0.0 copy-start.6
  55.7 0.0 copy-start.7
  55.7 0.8 collective-permute-done.4.other_ref
  56.5 0.0 all-to-all-done.1.kv_ref
  56.5 1.0 %shard_map.115 = bf16[8,48,256]{2,1,0:T(8,128)(2,1)S(1)} custom-call(bf16[4,48,128]{2,1,0:T(8,128)(2,1)S(1)} %pad_maximum_fusion.1.own_ref, bf16[4,48,128]{2,1,0:T(8,128)(2,1)S(1)} %collective-permute-done.4.other_ref, bf16[8,48,256]{2,1,0:T(8,128)(2,1)S(1)} %all-to-all-done.1.kv_ref), custom_call_target="tpu_custom_call" | custom-call | tf_op jit(solution)/shard_map/pallas_call | solution.py:340
  57.5 9.9 %all_to_all.20.o_ref = bf16[8,48,256]{2,1,0:T(8,128)(2,1)S(1)} all-to-all(bf16[8,48,256]{2,1,0:T(8,128)(2,1)S(1)} %shard_map.115), channel_id=1, replica_groups={{0,8,128,136,256,264,384,392},{16,24,144,152,272,280,400,408},{32,40,16..., dimensions={0} | all-to-all | bytes 393216 | tf_op jit(solution)/shard_map/all_to_all | solution.py:347
  67.4 0.0 copy-done.3
  67.4 1.1 %shard_map.116 = bf16[8,56,128]{2,1,0:T(8,128)(2,1)} custom-call(bf16[8,48,256]{2,1,0:T(8,128)(2,1)S(1)} %all_to_all.20.o_ref, bf16[128,1024]{1,0:T(8,128)(2,1)S(1)} %copy-done.3, bf16[8,128]{1,0:T(8,128)(2,1)S(1)} %pad_maximum_fusion.6.first_ref, bf16[8,128]{1,0:T(8,128)(2,1)S(1)} %pad_maximum_fusion.7.last_ref), custom_call_target="tpu_custom_call" | custom-call | tf_op jit(solution)/shard_map/pallas_call | solution.py:348
  68.5 13.9 %all-to-all-start.3 = ((bf16[8,56,128]{2,1,0:T(8,128)(2,1)}), bf16[8,56,128]{2,1,0:T(8,128)(2,1)S(1)}, u32[]{:S(2)}, u32[]{:S(2)}) async-start(bf16[8,56,128]{2,1,0:T(8,128)(2,1)} %shard_map.116), calls=%async_computation.3 | async-start | bytes 229376 | tf_op jit(solution)/shard_map/all_to_all | solution.py:354
  82.4 0.0 copy-done.1
  82.4 0.0 copy-done.2
  82.4 0.0 copy-done.6
  82.5 0.0 copy-done.7
  82.5 0.0 copy-start.5
  82.5 3.7 %shard_map.117.main_ref = bf16[12,180,128]{2,1,0:T(8,128)(2,1)S(1)} custom-call(bf16[12,180,128]{2,1,0:T(8,128)(2,1)S(1)} %bitcast.35, bf16[2,180,128]{2,1,0:T(8,128)(2,1)S(1)} %collective-permute-done.inner_ref, bf16[2,180,128]{2,1,0:T(8,128)(2,1)S(1)} %collective-permute-done.1.outer_ref, bf16[3,384,128]{2,1,0:T(8,128)(2,1)S(1)} %bitcast.36, ...), custom_call_target="tpu_custom_call" | custom-call | tf_op jit(solution)/shard_map/pallas_call | solution.py:363
  86.2 0.0 all-to-all-done.3.parts_ref
  86.2 0.0 copy-done.5
  86.2 1.4 %shard_map.118 = (bf16[48,128]{1,0:T(8,128)(2,1)}, bf16[12,180,128]{2,1,0:T(8,128)(2,1)}) custom-call(bf16[8,56,128]{2,1,0:T(8,128)(2,1)S(1)} %all-to-all-done.3.parts_ref, bf16[8,72,128]{2,1,0:T(8,128)(2,1)S(1)} %all-to-all-done.tokens_ref.incoming_ref, bf16[48,128]{1,0:T(8,128)(2,1)S(1)} %bitcast.41, bf16[12,180,128]{2,1,0:T(8,128)(2,1)S(1)} %shard_map.117.main_ref, ...), custom_call_target="tpu_custom_call" | custom-call | tf_op jit(solution)/shard_map/pallas_call | solution.py:373
  (19 shorter events, 0.2 us)
Async XLA Ops:
  1.6 0.7 copy-start.4
  3.0 26.9 %all-to-all-start = ((bf16[8,72,128]{2,1,0:T(8,128)(2,1)}), bf16[8,72,128]{2,1,0:T(8,128)(2,1)S(1)}, u32[]{:S(2)}, u32[]{:S(2)}) async-start(bf16[8,72,128]{2,1,0:T(8,128)(2,1)} %shard_map.113), calls=%async_computation | async-start | bytes 294912 | tf_op jit(solution)/shard_map/all_to_all | solution.py:306
  23.2 1.3 %copy-start = (bf16[1,12,180,128]{3,2,1,0:T(8,128)(2,1)S(1)}, bf16[1,12,180,128]{3,2,1,0:T(8,128)(2,1)}, u32[]{:S(2)}) copy-start(bf16[1,12,180,128]{3,2,1,0:T(8,128)(2,1)} %param.10) | copy-start | bytes 1658884
  24.5 21.2 %collective-permute-start.1 = (bf16[2,180,128]{2,1,0:T(8,128)(2,1)S(1)}, bf16[2,180,128]{2,1,0:T(8,128)(2,1)S(1)}, u32[]{:S(2)}, u32[]{:S(2)}) collective-permute-start(bf16[2,180,128]{2,1,0:T(8,128)(2,1)S(1)} %get-tuple-element.38), channel_id=1, source_target_pairs={{0,4},{1,5},{2,6},{3,7},{4,0},{5,1},{6,2},{7,3},{8,16},{9,17},{10,... | collective-permute-start | bytes 276488 | tf_op jit(solution)/shard_map/ppermute | solution.py:311
  28.0 17.7 %collective-permute-start = (bf16[2,180,128]{2,1,0:T(8,128)(2,1)S(1)}, bf16[2,180,128]{2,1,0:T(8,128)(2,1)S(1)}, u32[]{:S(2)}, u32[]{:S(2)}) collective-permute-start(bf16[2,180,128]{2,1,0:T(8,128)(2,1)S(1)} %get-tuple-element.39), channel_id=1, source_target_pairs={{0,8},{1,9},{2,10},{3,11},{4,12},{5,13},{6,14},{7,15},{8,0},{9,1},... | collective-permute-start | bytes 276488 | tf_op jit(solution)/shard_map/ppermute | solution.py:310
  31.0 14.8 %collective-permute-start.2 = (bf16[48,128]{1,0:T(8,128)(2,1)S(1)}, bf16[48,128]{1,0:T(8,128)(2,1)S(1)}, u32[]{:S(2)}, u32[]{:S(2)}) collective-permute-start(bf16[48,128]{1,0:T(8,128)(2,1)S(1)} %get-tuple-element.18), channel_id=1, source_target_pairs={{0,128},{8,136},{16,144},{24,152},{32,160},{40,168},{48,176},{56,1... | collective-permute-start | bytes 36872 | tf_op jit(solution)/shard_map/ppermute | solution.py:323
  39.1 17.4 %all-to-all-start.1 = ((bf16[8,48,256]{2,1,0:T(8,128)(2,1)}), bf16[8,48,256]{2,1,0:T(8,128)(2,1)S(1)}, u32[]{:S(2)}, u32[]{:S(2)}) async-start(bf16[8,48,256]{2,1,0:T(8,128)(2,1)} %get-tuple-element.23), calls=%async_computation.1 | async-start | bytes 393216 | tf_op jit(solution)/shard_map/all_to_all | solution.py:322
  45.7 21.7 %copy-start.3 = (bf16[128,1024]{1,0:T(8,128)(2,1)S(1)}, bf16[128,1024]{1,0:T(8,128)(2,1)}, u32[]{:S(2)}) copy-start(bf16[128,1024]{1,0:T(8,128)(2,1)} %wo_ref.1) | copy-start | bytes 786436
  45.8 6.2 %collective-permute-start.3 = (bf16[2,48,128]{2,1,0:T(8,128)(2,1)S(1)}, bf16[2,48,128]{2,1,0:T(8,128)(2,1)S(1)}, u32[]{:S(2)}, u32[]{:S(2)}) collective-permute-start(bf16[2,48,128]{2,1,0:T(8,128)(2,1)S(1)} %pad_maximum_fusion.2), channel_id=1, source_target_pairs={{0,384},{8,392},{16,400},{24,408},{32,416},{40,424},{48,432},{56,4... | collective-permute-start | bytes 73736 | tf_op jit(solution)/shard_map/ppermute | solution.py:323
  52.0 4.5 %collective-permute-start.4 = (bf16[4,48,128]{2,1,0:T(8,128)(2,1)S(1)}, bf16[4,48,128]{2,1,0:T(8,128)(2,1)S(1)}, u32[]{:S(2)}, u32[]{:S(2)}) collective-permute-start(bf16[4,48,128]{2,1,0:T(8,128)(2,1)S(1)} %pad_maximum_fusion.1.own_ref), channel_id=1, source_target_pairs={{0,8},{8,0},{16,24},{24,16},{32,40},{40,32},{48,56},{56,48},{64,72... | collective-permute-start | bytes 147464 | tf_op jit(solution)/shard_map/ppermute | solution.py:330
  55.6 26.8 %copy-start.1 = (bf16[3,3,128,128]{3,2,1,0:T(8,128)(2,1)S(1)}, bf16[3,3,128,128]{3,2,1,0:T(8,128)(2,1)}, u32[]{:S(2)}) copy-start(bf16[3,3,128,128]{3,2,1,0:T(8,128)(2,1)} %param.11) | copy-start | bytes 884740
  55.7 26.8 %copy-start.2 = (bf16[3,3,128,128]{3,2,1,0:T(8,128)(2,1)S(1)}, bf16[3,3,128,128]{3,2,1,0:T(8,128)(2,1)}, u32[]{:S(2)}) copy-start(bf16[3,3,128,128]{3,2,1,0:T(8,128)(2,1)} %param.14) | copy-start | bytes 884740
  55.7 26.8 %copy-start.6 = (f32[2,128]{1,0:T(2,128)S(1)}, f32[2,128]{1,0:T(2,128)}, u32[]{:S(2)}) copy-start(f32[2,128]{1,0:T(2,128)} %film_ref.3) | copy-start | bytes 3076
  55.7 26.8 %copy-start.7 = (f32[128]{0:T(128)S(1)}, f32[128]{0:T(128)}, u32[]{:S(2)}) copy-start(f32[128]{0:T(128)} %param.12) | copy-start | bytes 1540
  68.5 17.6 %all-to-all-start.3 = ((bf16[8,56,128]{2,1,0:T(8,128)(2,1)}), bf16[8,56,128]{2,1,0:T(8,128)(2,1)S(1)}, u32[]{:S(2)}, u32[]{:S(2)}) async-start(bf16[8,56,128]{2,1,0:T(8,128)(2,1)} %shard_map.116), calls=%async_computation.3 | async-start | bytes 229376 | tf_op jit(solution)/shard_map/all_to_all | solution.py:354
  82.5 3.7 %copy-start.5 = (bf16[1,48,128]{2,1,0:T(8,128)(2,1)S(1)}, bf16[1,48,128]{2,1,0:T(8,128)(2,1)}, u32[]{:S(2)}) copy-start(bf16[1,48,128]{2,1,0:T(8,128)(2,1)} %param.15) | copy-start | bytes 36868

commit v5 on v4

--- a/solution.py
+++ b/solution.py
@@ -295,7 +295,7 @@
     column = lambda c: field[:, c]
     spread = pl.pallas_call(
         spread_body,
-        in_specs=[pl.BlockSpec(memory_space=pl.ANY), vmem],
+        in_specs=[pl.BlockSpec(memory_space=pltpu.HBM), vmem],
         out_shape=jax.ShapeDtypeStruct((lons, rows + 2 * height, channels), BF16),
         scratch_shapes=[pltpu.VMEM(tokens.shape, BF16), pltpu.SemaphoreType.DMA],
         compiler_params=params,

time: 88.4 us -> 88.4 us (level)
  no operation moved by 1% of the time
where the time goes in v5:
time: 88.4 us; the launch traced here: 87.7 us
  starting transfers between devices  61.7 us (70%)
  blocking collectives  9.89 us (11%)
  Pallas kernels  8.96 us (10%)
  waiting for transfers between devices  3.01 us (3%)
  local copies, waits for them, and re-layouts  1.77 us (2%)
  other arithmetic  1.41 us (2%)
  between operations  0.95 us (1%)
    all_to_all x1, starting transfers between devices, shards(): incoming = lax.all_to_all(spread, 'lon', 0, 0, axis_index_groups=turned)  20.1 us
    all_to_all x1, starting transfers between devices, shards(): projected = lax.all_to_all(projected, 'lon', 0, 0, axis_index_groups=turned)  13.9 us
    ppermute x2, starting transfers between devices, shards(): lax.ppermute(v, 'lat', [(i, to(i // step) * step + i % step) for i in ran...  12 us
    all_to_all x1, blocking collectives, shards(): partial = lax.all_to_all(partial, 'lat', 0, 0, axis_index_groups=over_xc)  9.89 us
    all_to_all x1, starting transfers between devices, shards(): pairs = lax.all_to_all(pairs, 'lat', 0, 0, axis_index_groups=over_z)  6.66 us
    pallas_call x1, Pallas kernels, shards(): pl.pallas_call(conv_body, in_specs=[vmem] * 7, out_shape=jax.ShapeDtypeSt...  3.67 us
    ppermute x1, starting transfers between devices, shards(): other = lax.ppermute(own, 'lat', [(i, i ^ 1) for i in range(lats)])  3.62 us
    ppermute x1, starting transfers between devices, shards(): lax.ppermute(jnp.where(even, upper, lower), ('lat', 'lon'), outer)  3.49 us
  transfers between devices with their start and end apart: 8, of which 2 were waited for; matrix products, arithmetic and copies ran while one was open for 2% of the time, Pallas kernels for 5%

profile of v5, /device:TPU:1, one launch (start us, length us, event | category | flops | bytes accessed | tf_op | source)
XLA Modules:
  0.0 87.7 jit_solution(10648374323742950269)
XLA Ops:
  0.6 1.0 %fusion.2 = (bf16[12,1,128]{2,1,0:T(2,128)(2,1)S(1)}, bf16[12,1,128]{2,1,0:T(2,128)(2,1)S(1)}, bf16[12,1,128]{2,1,0:T(2,128)(2,1)S(1)}, bf16[12,1,128]{2,1,0:T(2,128)(2,1)S(1)}) fusion(bf16[12,180,128]{2,1,0:T(8,128)(2,1)} %bitcast.33), kind=kLoop, calls=%fused_computation.28 | loop fusion | bytes 24576 | tf_op jit(solution)/shard_map/slice | solution.py:295
  1.6 0.0 copy-start.4
  1.6 0.7 copy-done.4
  2.3 0.7 shard_map.113
  3.0 20.1 %all-to-all-start = ((bf16[8,72,128]{2,1,0:T(8,128)(2,1)}), bf16[8,72,128]{2,1,0:T(8,128)(2,1)S(1)}, u32[]{:S(2)}, u32[]{:S(2)}) async-start(bf16[8,72,128]{2,1,0:T(8,128)(2,1)} %shard_map.113), calls=%async_computation | async-start | bytes 294912 | tf_op jit(solution)/shard_map/all_to_all | solution.py:306
  23.2 0.0 copy-start
  23.2 1.3 %pad_maximum_fusion.weight_ref = bf16[1024,384]{1,0:T(8,128)(2,1)S(1)} fusion(bf16[1024,128]{1,0:T(8,128)(2,1)} %param.18, bf16[1024,128]{1,0:T(8,128)(2,1)} %param.17, bf16[1024,128]{1,0:T(8,128)(2,1)} %param.16), kind=kLoop, calls=%fused_computation | loop fusion | flops 2359296 | bytes 1572864 | tf_op jit(solution)/shard_map/concatenate | solution.py:308
  24.5 0.0 copy-done
  24.5 3.5 %collective-permute-start.1 = (bf16[2,180,128]{2,1,0:T(8,128)(2,1)S(1)}, bf16[2,180,128]{2,1,0:T(8,128)(2,1)S(1)}, u32[]{:S(2)}, u32[]{:S(2)}) collective-permute-start(bf16[2,180,128]{2,1,0:T(8,128)(2,1)S(1)} %get-tuple-element.38), channel_id=1, source_target_pairs={{0,4},{1,5},{2,6},{3,7},{4,0},{5,1},{6,2},{7,3},{8,16},{9,17},{10,... | collective-permute-start | bytes 276488 | tf_op jit(solution)/shard_map/ppermute | solution.py:311
  28.0 1.9 %collective-permute-start = (bf16[2,180,128]{2,1,0:T(8,128)(2,1)S(1)}, bf16[2,180,128]{2,1,0:T(8,128)(2,1)S(1)}, u32[]{:S(2)}, u32[]{:S(2)}) collective-permute-start(bf16[2,180,128]{2,1,0:T(8,128)(2,1)S(1)} %get-tuple-element.39), channel_id=1, source_target_pairs={{0,8},{1,9},{2,10},{3,11},{4,12},{5,13},{6,14},{7,15},{8,0},{9,1},... | collective-permute-start | bytes 276488 | tf_op jit(solution)/shard_map/ppermute | solution.py:310
  30.0 0.0 all-to-all-done.tokens_ref.incoming_ref
  30.0 1.0 %shard_map.114 = (bf16[48,128]{1,0:T(8,128)(2,1)S(1)}, bf16[8,48,256]{2,1,0:T(8,128)(2,1)}) custom-call(bf16[8,72,128]{2,1,0:T(8,128)(2,1)S(1)} %all-to-all-done.tokens_ref.incoming_ref, bf16[1024,384]{1,0:T(8,128)(2,1)S(1)} %pad_maximum_fusion.weight_ref), custom_call_target="tpu_custom_call" | custom-call | tf_op jit(solution)/shard_map/pallas_call | solution.py:315
  31.0 8.1 %collective-permute-start.2 = (bf16[48,128]{1,0:T(8,128)(2,1)S(1)}, bf16[48,128]{1,0:T(8,128)(2,1)S(1)}, u32[]{:S(2)}, u32[]{:S(2)}) collective-permute-start(bf16[48,128]{1,0:T(8,128)(2,1)S(1)} %get-tuple-element.18), channel_id=1, source_target_pairs={{0,128},{8,136},{16,144},{24,152},{32,160},{40,168},{48,176},{56,1... | collective-permute-start | bytes 36872 | tf_op jit(solution)/shard_map/ppermute | solution.py:323
  39.1 6.7 %all-to-all-start.1 = ((bf16[8,48,256]{2,1,0:T(8,128)(2,1)}), bf16[8,48,256]{2,1,0:T(8,128)(2,1)S(1)}, u32[]{:S(2)}, u32[]{:S(2)}) async-start(bf16[8,48,256]{2,1,0:T(8,128)(2,1)} %get-tuple-element.23), calls=%async_computation.1 | async-start | bytes 393216 | tf_op jit(solution)/shard_map/all_to_all | solution.py:322
  45.7 0.0 copy-start.3
  45.7 0.0 collective-permute-done.1.outer_ref
  45.8 0.0 collective-permute-done.inner_ref
  45.8 0.0 collective-permute-done.2
  45.8 3.9 %collective-permute-start.3 = (bf16[2,48,128]{2,1,0:T(8,128)(2,1)S(1)}, bf16[2,48,128]{2,1,0:T(8,128)(2,1)S(1)}, u32[]{:S(2)}, u32[]{:S(2)}) collective-permute-start(bf16[2,48,128]{2,1,0:T(8,128)(2,1)S(1)} %pad_maximum_fusion.2), channel_id=1, source_target_pairs={{0,384},{8,392},{16,400},{24,408},{32,416},{40,424},{48,432},{56,4... | collective-permute-start | bytes 73736 | tf_op jit(solution)/shard_map/ppermute | solution.py:323
  49.8 2.2 %collective-permute-done.3 = bf16[2,48,128]{2,1,0:T(8,128)(2,1)S(1)} collective-permute-done((bf16[2,48,128]{2,1,0:T(8,128)(2,1)S(1)}, bf16[2,48,128]{2,1,0:T(8,128)(2,1)S(1)}, u32[]{:S(2)}, u32[]{:S(2)}) %collective-permute-start.3) | collective-permute-done | bytes 24608 | tf_op jit(solution)/shard_map/ppermute | solution.py:323
  52.0 3.6 %collective-permute-start.4 = (bf16[4,48,128]{2,1,0:T(8,128)(2,1)S(1)}, bf16[4,48,128]{2,1,0:T(8,128)(2,1)S(1)}, u32[]{:S(2)}, u32[]{:S(2)}) collective-permute-start(bf16[4,48,128]{2,1,0:T(8,128)(2,1)S(1)} %pad_maximum_fusion.1.own_ref), channel_id=1, source_target_pairs={{0,8},{8,0},{16,24},{24,16},{32,40},{40,32},{48,56},{56,48},{64,72... | collective-permute-start | bytes 147464 | tf_op jit(solution)/shard_map/ppermute | solution.py:330
  55.6 0.0 copy-start.1
  55.7 0.0 copy-start.2
  55.7 0.0 copy-start.6
  55.7 0.0 copy-start.7
  55.7 0.8 collective-permute-done.4.other_ref
  56.5 0.0 all-to-all-done.1.kv_ref
  56.5 1.0 %shard_map.115 = bf16[8,48,256]{2,1,0:T(8,128)(2,1)S(1)} custom-call(bf16[4,48,128]{2,1,0:T(8,128)(2,1)S(1)} %pad_maximum_fusion.1.own_ref, bf16[4,48,128]{2,1,0:T(8,128)(2,1)S(1)} %collective-permute-done.4.other_ref, bf16[8,48,256]{2,1,0:T(8,128)(2,1)S(1)} %all-to-all-done.1.kv_ref), custom_call_target="tpu_custom_call" | custom-call | tf_op jit(solution)/shard_map/pallas_call | solution.py:340
  57.5 9.9 %all_to_all.20.o_ref = bf16[8,48,256]{2,1,0:T(8,128)(2,1)S(1)} all-to-all(bf16[8,48,256]{2,1,0:T(8,128)(2,1)S(1)} %shard_map.115), channel_id=1, replica_groups={{0,8,128,136,256,264,384,392},{16,24,144,152,272,280,400,408},{32,40,16..., dimensions={0} | all-to-all | bytes 393216 | tf_op jit(solution)/shard_map/all_to_all | solution.py:347
  67.4 0.0 copy-done.3
  67.4 1.1 %shard_map.116 = bf16[8,56,128]{2,1,0:T(8,128)(2,1)} custom-call(bf16[8,48,256]{2,1,0:T(8,128)(2,1)S(1)} %all_to_all.20.o_ref, bf16[128,1024]{1,0:T(8,128)(2,1)S(1)} %copy-done.3, bf16[8,128]{1,0:T(8,128)(2,1)S(1)} %pad_maximum_fusion.6.first_ref, bf16[8,128]{1,0:T(8,128)(2,1)S(1)} %pad_maximum_fusion.7.last_ref), custom_call_target="tpu_custom_call" | custom-call | tf_op jit(solution)/shard_map/pallas_call | solution.py:348
  68.5 13.9 %all-to-all-start.3 = ((bf16[8,56,128]{2,1,0:T(8,128)(2,1)}), bf16[8,56,128]{2,1,0:T(8,128)(2,1)S(1)}, u32[]{:S(2)}, u32[]{:S(2)}) async-start(bf16[8,56,128]{2,1,0:T(8,128)(2,1)} %shard_map.116), calls=%async_computation.3 | async-start | bytes 229376 | tf_op jit(solution)/shard_map/all_to_all | solution.py:354
  82.4 0.0 copy-done.1
  82.4 0.0 copy-done.2
  82.4 0.0 copy-done.6
  82.5 0.0 copy-done.7
  82.5 0.0 copy-start.5
  82.5 3.7 %shard_map.117.main_ref = bf16[12,180,128]{2,1,0:T(8,128)(2,1)S(1)} custom-call(bf16[12,180,128]{2,1,0:T(8,128)(2,1)S(1)} %bitcast.35, bf16[2,180,128]{2,1,0:T(8,128)(2,1)S(1)} %collective-permute-done.inner_ref, bf16[2,180,128]{2,1,0:T(8,128)(2,1)S(1)} %collective-permute-done.1.outer_ref, bf16[3,384,128]{2,1,0:T(8,128)(2,1)S(1)} %bitcast.36, ...), custom_call_target="tpu_custom_call" | custom-call | tf_op jit(solution)/shard_map/pallas_call | solution.py:363
  86.2 0.0 all-to-all-done.3.parts_ref
  86.2 0.0 copy-done.5
  86.2 1.4 %shard_map.118 = (bf16[48,128]{1,0:T(8,128)(2,1)}, bf16[12,180,128]{2,1,0:T(8,128)(2,1)}) custom-call(bf16[8,56,128]{2,1,0:T(8,128)(2,1)S(1)} %all-to-all-done.3.parts_ref, bf16[8,72,128]{2,1,0:T(8,128)(2,1)S(1)} %all-to-all-done.tokens_ref.incoming_ref, bf16[48,128]{1,0:T(8,128)(2,1)S(1)} %bitcast.41, bf16[12,180,128]{2,1,0:T(8,128)(2,1)S(1)} %shard_map.117.main_ref, ...), custom_call_target="tpu_custom_call" | custom-call | tf_op jit(solution)/shard_map/pallas_call | solution.py:373
  (19 shorter events, 0.2 us)
Async XLA Ops:
  1.6 0.7 copy-start.4
  3.0 26.9 %all-to-all-start = ((bf16[8,72,128]{2,1,0:T(8,128)(2,1)}), bf16[8,72,128]{2,1,0:T(8,128)(2,1)S(1)}, u32[]{:S(2)}, u32[]{:S(2)}) async-start(bf16[8,72,128]{2,1,0:T(8,128)(2,1)} %shard_map.113), calls=%async_computation | async-start | bytes 294912 | tf_op jit(solution)/shard_map/all_to_all | solution.py:306
  23.2 1.3 %copy-start = (bf16[1,12,180,128]{3,2,1,0:T(8,128)(2,1)S(1)}, bf16[1,12,180,128]{3,2,1,0:T(8,128)(2,1)}, u32[]{:S(2)}) copy-start(bf16[1,12,180,128]{3,2,1,0:T(8,128)(2,1)} %param.10) | copy-start | bytes 1658884
  24.5 21.2 %collective-permute-start.1 = (bf16[2,180,128]{2,1,0:T(8,128)(2,1)S(1)}, bf16[2,180,128]{2,1,0:T(8,128)(2,1)S(1)}, u32[]{:S(2)}, u32[]{:S(2)}) collective-permute-start(bf16[2,180,128]{2,1,0:T(8,128)(2,1)S(1)} %get-tuple-element.38), channel_id=1, source_target_pairs={{0,4},{1,5},{2,6},{3,7},{4,0},{5,1},{6,2},{7,3},{8,16},{9,17},{10,... | collective-permute-start | bytes 276488 | tf_op jit(solution)/shard_map/ppermute | solution.py:311
  28.0 17.7 %collective-permute-start = (bf16[2,180,128]{2,1,0:T(8,128)(2,1)S(1)}, bf16[2,180,128]{2,1,0:T(8,128)(2,1)S(1)}, u32[]{:S(2)}, u32[]{:S(2)}) collective-permute-start(bf16[2,180,128]{2,1,0:T(8,128)(2,1)S(1)} %get-tuple-element.39), channel_id=1, source_target_pairs={{0,8},{1,9},{2,10},{3,11},{4,12},{5,13},{6,14},{7,15},{8,0},{9,1},... | collective-permute-start | bytes 276488 | tf_op jit(solution)/shard_map/ppermute | solution.py:310
  31.0 14.8 %collective-permute-start.2 = (bf16[48,128]{1,0:T(8,128)(2,1)S(1)}, bf16[48,128]{1,0:T(8,128)(2,1)S(1)}, u32[]{:S(2)}, u32[]{:S(2)}) collective-permute-start(bf16[48,128]{1,0:T(8,128)(2,1)S(1)} %get-tuple-element.18), channel_id=1, source_target_pairs={{0,128},{8,136},{16,144},{24,152},{32,160},{40,168},{48,176},{56,1... | collective-permute-start | bytes 36872 | tf_op jit(solution)/shard_map/ppermute | solution.py:323
  39.1 17.4 %all-to-all-start.1 = ((bf16[8,48,256]{2,1,0:T(8,128)(2,1)}), bf16[8,48,256]{2,1,0:T(8,128)(2,1)S(1)}, u32[]{:S(2)}, u32[]{:S(2)}) async-start(bf16[8,48,256]{2,1,0:T(8,128)(2,1)} %get-tuple-element.23), calls=%async_computation.1 | async-start | bytes 393216 | tf_op jit(solution)/shard_map/all_to_all | solution.py:322
  45.7 21.7 %copy-start.3 = (bf16[128,1024]{1,0:T(8,128)(2,1)S(1)}, bf16[128,1024]{1,0:T(8,128)(2,1)}, u32[]{:S(2)}) copy-start(bf16[128,1024]{1,0:T(8,128)(2,1)} %wo_ref.1) | copy-start | bytes 786436
  45.8 6.2 %collective-permute-start.3 = (bf16[2,48,128]{2,1,0:T(8,128)(2,1)S(1)}, bf16[2,48,128]{2,1,0:T(8,128)(2,1)S(1)}, u32[]{:S(2)}, u32[]{:S(2)}) collective-permute-start(bf16[2,48,128]{2,1,0:T(8,128)(2,1)S(1)} %pad_maximum_fusion.2), channel_id=1, source_target_pairs={{0,384},{8,392},{16,400},{24,408},{32,416},{40,424},{48,432},{56,4... | collective-permute-start | bytes 73736 | tf_op jit(solution)/shard_map/ppermute | solution.py:323
  52.0 4.5 %collective-permute-start.4 = (bf16[4,48,128]{2,1,0:T(8,128)(2,1)S(1)}, bf16[4,48,128]{2,1,0:T(8,128)(2,1)S(1)}, u32[]{:S(2)}, u32[]{:S(2)}) collective-permute-start(bf16[4,48,128]{2,1,0:T(8,128)(2,1)S(1)} %pad_maximum_fusion.1.own_ref), channel_id=1, source_target_pairs={{0,8},{8,0},{16,24},{24,16},{32,40},{40,32},{48,56},{56,48},{64,72... | collective-permute-start | bytes 147464 | tf_op jit(solution)/shard_map/ppermute | solution.py:330
  55.6 26.8 %copy-start.1 = (bf16[3,3,128,128]{3,2,1,0:T(8,128)(2,1)S(1)}, bf16[3,3,128,128]{3,2,1,0:T(8,128)(2,1)}, u32[]{:S(2)}) copy-start(bf16[3,3,128,128]{3,2,1,0:T(8,128)(2,1)} %param.11) | copy-start | bytes 884740
  55.7 26.8 %copy-start.2 = (bf16[3,3,128,128]{3,2,1,0:T(8,128)(2,1)S(1)}, bf16[3,3,128,128]{3,2,1,0:T(8,128)(2,1)}, u32[]{:S(2)}) copy-start(bf16[3,3,128,128]{3,2,1,0:T(8,128)(2,1)} %param.14) | copy-start | bytes 884740
  55.7 26.8 %copy-start.6 = (f32[2,128]{1,0:T(2,128)S(1)}, f32[2,128]{1,0:T(2,128)}, u32[]{:S(2)}) copy-start(f32[2,128]{1,0:T(2,128)} %film_ref.3) | copy-start | bytes 3076
  55.7 26.8 %copy-start.7 = (f32[128]{0:T(128)S(1)}, f32[128]{0:T(128)}, u32[]{:S(2)}) copy-start(f32[128]{0:T(128)} %param.12) | copy-start | bytes 1540
  68.5 17.6 %all-to-all-start.3 = ((bf16[8,56,128]{2,1,0:T(8,128)(2,1)}), bf16[8,56,128]{2,1,0:T(8,128)(2,1)S(1)}, u32[]{:S(2)}, u32[]{:S(2)}) async-start(bf16[8,56,128]{2,1,0:T(8,128)(2,1)} %shard_map.116), calls=%async_computation.3 | async-start | bytes 229376 | tf_op jit(solution)/shard_map/all_to_all | solution.py:354
  82.5 3.7 %copy-start.5 = (bf16[1,48,128]{2,1,0:T(8,128)(2,1)S(1)}, bf16[1,48,128]{2,1,0:T(8,128)(2,1)}, u32[]{:S(2)}) copy-start(bf16[1,48,128]{2,1,0:T(8,128)(2,1)} %param.15) | copy-start | bytes 36868
